TPU v7x, 512 devices: a whole 4x8x8 slice. The times are simulated.
512 devices in a mesh: rows: 32 (over z_hi, x, core), cols: 16 (over y, z_lo).
Axes of the slice: x: 4, y: 8, z: 8 (z_hi: 4, z_lo: 2; z = z_hi * 2 + z_lo), core: 2. Of those that a mesh axis runs over, the one named last changes fastest.
Arguments:
- tokens: bfloat16 [416, 2048], P(None, 'rows'), may hold values from -24 to 24
- arrival: int32 [416], replicated, may hold values from 0 to 415, each once
- cache_lengths: int32 [416], replicated, may hold values from 1 to 1023, as said below
- move_slot: int32 [32, 4], replicated, may hold values from 0 to 12, as said below
- move_target: int32 [32, 4], replicated, may hold values from 0 to 31, as said below
- page_table: int32 [32, 16, 13, 2], P('rows', 'cols'), may hold values from 0 to 25, as said below
- kv_pool: bfloat16 [832, 16, 32, 512], P('rows', 'cols'), may hold values from -400 to 400
- ssm_state: bfloat16 [416, 32, 64, 256], P('rows', 'cols'), may hold values from -1.5 to 1.5
- conv_x: bfloat16 [416, 3, 2048], P('rows', None, 'cols'), may hold values from -6 to 6
- conv_bc: bfloat16 [416, 3, 512], P('rows'), may hold values from -6 to 6
- norm_gain: bfloat16 [2048], P('rows'), may hold values from 0.099609375 to 1.8984375
- weight_z: bfloat16 [2048, 2048], P('rows', 'cols'), may hold values from -0.125 to 0.125
- weight_x: bfloat16 [2048, 2048], P('rows', 'cols'), may hold values from -0.125 to 0.125
- weight_dt: bfloat16 [2048, 32], P('rows', 'cols'), may hold values from -0.125 to 0.125
- weight_bc: bfloat16 [2048, 512], P('rows'), may hold values from -0.125 to 0.125
- weight_qkv: bfloat16 [2048, 1536], P('rows'), may hold values from -0.125 to 0.125
- conv_weight_x: bfloat16 [4, 2048], P(None, 'cols'), may hold values from -3 to 3
- conv_weight_bc: bfloat16 [4, 512], replicated, may hold values from -3 to 3
- dt_bias: float32 [32], P('cols'), may hold values from -4 to -1
- a_log: float32 [32], P('cols'), may hold values from 0 to 2.5
- d_skip: float32 [32], P('cols'), may hold values from 0.5 to 1.5
- weight_ssm_out: bfloat16 [2048, 2048], P('cols'), may hold values from -0.125 to 0.125
- weight_attn_out: bfloat16 [1024, 2048], P('cols'), may hold values from -0.1875 to 0.1875
Outputs:
- mixed: bfloat16 [416, 2048], P('rows', 'cols')
- ssm_next: bfloat16 [416, 32, 64, 256], P('rows', 'cols')
- conv_x_next: bfloat16 [416, 3, 2048], P('rows', None, 'cols')
- conv_bc_next: bfloat16 [416, 3, 512], P('rows')
- kv_next: bfloat16 [832, 16, 32, 512], P('rows', 'cols')
Inputs may be any that keep to these rules, and one draw needn't show every extreme that they name: `cache_lengths`: some request has 1023 cached tokens. `move_slot`: each row lists 4 distinct slots. `move_target`: each row lists 4 distinct row indices other than its own; every row index is named exactly 4 times, by distinct sources. `page_table`: the 13 x 2 entries of one device are each of 0 to 25 once.
All inputs are finite; a program needn't handle non-finite values.
Results may differ from a plain program's by a relative error of at most 0.011.
Values may be sent and summed in bfloat16 or wider, within the bound.
A program may use at most 64 MiB of HBM per device.

v0:
```python
import jax
import jax.numpy as jnp
from jax import lax
from jax.sharding import PartitionSpec as P

D = 2048
HP = 64
NS = 256
QH = 8
KVH = 2
HD = 128
PAGE = 32


EPSILON = 1e-05
FLOOR_SCORE = -1e30
PRECISE = lax.Precision.HIGHEST


def merged(value, axis, combine):
    everything = jax.tree.map(lambda part: lax.all_gather(part, axis), value)
    initial = jax.tree.map(lambda part: part[0], everything)

    def step(k, so_far):
        return combine(so_far, jax.tree.map(lambda part: part[k], everything))

    return lax.fori_loop(1, lax.axis_size(axis), step, initial)


def residents(move_slot, move_target, row_count, slot_count):
    move_count = move_slot.shape[1]
    devices = jnp.arange(row_count, dtype=jnp.int32)
    matches = move_target[:, None, :] == devices[None, :, None]
    sending = jnp.any(matches, axis=2)
    slot_from = jnp.sum(jnp.where(matches, move_slot[:, None, :], 0), axis=2)
    ranking = jnp.cumsum(sending.astype(jnp.int32), axis=0) - 1
    leaving = devices[:, None] * slot_count + slot_from
    turn_order = jnp.arange(move_count, dtype=jnp.int32)
    chosen = sending[:, :, None] & (ranking[:, :, None] == turn_order[None, None, :])
    incoming = jnp.sum(jnp.where(chosen, leaving[:, :, None], 0), axis=0)
    places = jnp.arange(slot_count, dtype=jnp.int32)
    vacant = move_slot[:, :, None] == places[None, None, :]
    filled = jnp.sum(jnp.where(vacant, incoming[:, :, None], 0), axis=1)
    staying = devices[:, None] * slot_count + places[None, :]
    return jnp.where(jnp.any(vacant, axis=1), filled, staying)


def outgoing_slots(move_slot, move_target, row_index, row_count):
    targets_here = lax.dynamic_index_in_dim(move_target, row_index, 0, keepdims=False)
    slots_here = lax.dynamic_index_in_dim(move_slot, row_index, 0, keepdims=False)
    peer_index = jnp.arange(row_count, dtype=jnp.int32)
    matches = targets_here[None, :] == peer_index[:, None]
    return jnp.sum(jnp.where(matches, slots_here[None, :], 0), axis=1)


def arrival_index(layout, row_index, slot_count):
    resident = lax.dynamic_index_in_dim(layout, row_index, 0, keepdims=False)
    anchor = resident // slot_count
    return jnp.where(
        anchor == row_index, jnp.arange(slot_count, dtype=jnp.int32), slot_count + anchor
    )


def migrate(members, sending, placing):
    state_part, conv_x_part, conv_bc_part, pages_part = members
    arrived = (
        lax.all_to_all(
            jnp.take(state_part, sending, axis=0), "rows", split_axis=0, concat_axis=0, tiled=True
        ),
        lax.all_to_all(
            jnp.take(conv_x_part, sending, axis=0), "rows", split_axis=0, concat_axis=0, tiled=True
        ),
        lax.all_to_all(
            jnp.take(conv_bc_part, sending, axis=0), "rows", split_axis=0, concat_axis=0, tiled=True
        ),
        lax.all_to_all(
            jnp.take(pages_part, sending, axis=0), "rows", split_axis=0, concat_axis=0, tiled=True
        ),
    )
    return tuple(
        (
            jnp.take(jnp.concatenate([resident_part, arrived_part], axis=0), placing, axis=0)
            for resident_part, arrived_part in zip(members, arrived)
        )
    )


def combine(first_part, second_part):
    joint_peak = jnp.maximum(first_part[0], second_part[0])
    first_scale = jnp.exp(first_part[0] - joint_peak)
    second_scale = jnp.exp(second_part[0] - joint_peak)
    joint_total = first_part[1] * first_scale + second_part[1] * second_scale
    joint_sum = first_part[2] * first_scale[..., None] + second_part[2] * second_scale[..., None]
    return (joint_peak, joint_total, joint_sum)


def serve_rows(
    projected,
    state_part,
    conv_x_part,
    conv_bc_part,
    pages_part,
    lengths_here,
    conv_weight_x,
    conv_weight_bc,
    dt_bias,
    a_log,
    d_skip,
    col_index,
    col_count,
):
    slot_count = projected.shape[0]
    head_count = dt_bias.shape[0]
    inner_width = head_count * HP
    bc_start = 2 * inner_width + head_count
    gate_in = projected[:, :inner_width]
    value_in = projected[:, inner_width : 2 * inner_width]
    step_in = projected[:, 2 * inner_width : bc_start]
    bc_in = projected[:, bc_start : bc_start + 2 * NS]
    qkv_in = projected[:, bc_start + 2 * NS :]
    window_x = jnp.concatenate([conv_x_part, value_in[:, None, :]], axis=1)
    window_bc = jnp.concatenate([conv_bc_part, bc_in[:, None, :]], axis=1)
    value_act = jax.nn.silu(
        jnp.sum(window_x.astype(jnp.float32) * conv_weight_x.astype(jnp.float32)[None], axis=1)
    )
    bc_act = jax.nn.silu(
        jnp.sum(window_bc.astype(jnp.float32) * conv_weight_bc.astype(jnp.float32)[None], axis=1)
    ).astype(jnp.bfloat16)
    b_in = bc_act[:, :NS].astype(jnp.float32)
    c_out = bc_act[:, NS:].astype(jnp.float32)
    step_size = jax.nn.softplus(step_in.astype(jnp.float32) + dt_bias[None, :])
    decay_rate = jnp.exp(-jnp.exp(a_log)[None, :] * step_size)
    value_heads = value_act.reshape(slot_count, head_count, HP)
    state_new = (
        decay_rate[:, :, None, None] * state_part.astype(jnp.float32)
        + (step_size[:, :, None] * value_heads)[:, :, :, None] * b_in[:, None, None, :]
    )
    readout = (
        jnp.einsum("shpn,sn->shp", state_new, c_out, precision=PRECISE)
        + d_skip[None, :, None] * value_heads
    )
    gated = (
        readout.reshape(slot_count, inner_width) * jax.nn.silu(gate_in.astype(jnp.float32))
    ).astype(jnp.bfloat16)
    group_size = QH // KVH
    queries = qkv_in[:, : QH * HD].reshape(slot_count, KVH, group_size, HD)
    key_new = qkv_in[:, QH * HD : (QH + KVH) * HD]
    value_new = qkv_in[:, (QH + KVH) * HD :]
    pages_here = pages_part.shape[1]
    width = pages_part.shape[3]
    cached = pages_part.reshape(slot_count, pages_here * PAGE, width)
    cached_keys = cached[:, :, : KVH * HD].reshape(slot_count, pages_here * PAGE, KVH, HD)
    cached_values = cached[:, :, KVH * HD :].reshape(slot_count, pages_here * PAGE, KVH, HD)
    local_page = jnp.arange(pages_here, dtype=jnp.int32)[:, None]
    offsets = jnp.arange(PAGE, dtype=jnp.int32)[None, :]
    positions = ((local_page * col_count + col_index) * PAGE + offsets).reshape(-1)
    live_mask = (positions[None, :] < lengths_here[:, None])[:, None, None, :]
    score_scale = HD ** (-0.5)
    scores = (
        jnp.einsum("skgd,stkd->skgt", queries, cached_keys, preferred_element_type=jnp.float32)
        * score_scale
    )
    local_peak = jnp.max(jnp.where(live_mask, scores, FLOOR_SCORE), axis=3)
    weights = jnp.where(live_mask, jnp.exp(scores - local_peak[..., None]), 0.0)
    local_total = jnp.sum(weights, axis=3)
    summed = jnp.einsum(
        "skgt,stkd->skgd", weights, cached_values.astype(jnp.float32), precision=PRECISE
    )
    logical = lengths_here // PAGE
    owner_col = logical % col_count
    write_page = logical // col_count
    write_off = lengths_here % PAGE
    fresh_rows = jnp.concatenate([key_new, value_new], axis=1)
    write_mask = (
        (owner_col == col_index)[:, None, None]
        & (jnp.arange(pages_here, dtype=jnp.int32)[None, :, None] == write_page[:, None, None])
        & (jnp.arange(PAGE, dtype=jnp.int32)[None, None, :] == write_off[:, None, None])
    )
    pages_next = jnp.where(write_mask[..., None], fresh_rows[:, None, None, :], pages_part)
    results = (state_new.astype(jnp.bfloat16), window_x[:, 1:], window_bc[:, 1:], pages_next)
    partials = (local_peak, local_total, summed)
    fresh_parts = (
        queries,
        key_new.reshape(slot_count, KVH, HD),
        value_new.reshape(slot_count, KVH, HD),
    )
    return (results, partials, fresh_parts, gated)


def local(
    tokens,
    arrival,
    cache_lengths,
    move_slot,
    move_target,
    page_table,
    kv_pool,
    ssm_state,
    conv_x,
    conv_bc,
    norm_gain,
    weight_z,
    weight_x,
    weight_dt,
    weight_bc,
    weight_qkv,
    conv_weight_x,
    conv_weight_bc,
    dt_bias,
    a_log,
    d_skip,
    weight_ssm_out,
    weight_attn_out,
):
    row_count = lax.axis_size("rows")
    col_count = lax.axis_size("cols")
    row_index = lax.axis_index("rows")
    col_index = lax.axis_index("cols")
    slot_count = ssm_state.shape[0]
    total_rows = tokens.shape[0]
    pages_here = page_table.shape[3]
    width = kv_pool.shape[3]
    layout = residents(move_slot, move_target, row_count, slot_count)
    sending = outgoing_slots(move_slot, move_target, row_index, row_count)
    placing = arrival_index(layout, row_index, slot_count)
    inverse = (
        jnp.zeros((total_rows,), jnp.int32).at[arrival].set(jnp.arange(total_rows, dtype=jnp.int32))
    )
    picked = jnp.take(tokens, inverse[layout.reshape(-1)], axis=0)
    widened = picked.astype(jnp.float32)
    squares = jnp.sum(jnp.square(widened), axis=1)
    scaled = (widened * norm_gain.astype(jnp.float32)[None, :]).astype(jnp.bfloat16)
    weights_in = jnp.concatenate([weight_z, weight_x, weight_dt, weight_bc, weight_qkv], axis=1)
    partial_terms = jnp.dot(scaled, weights_in, preferred_element_type=jnp.float32)
    summed, square_sum = (
        lax.psum_scatter(partial_terms, "rows", scatter_dimension=0, tiled=True),
        lax.psum_scatter(squares, "rows", scatter_dimension=0, tiled=True),
    )
    projected = (summed / jnp.sqrt(square_sum / D + EPSILON)[:, None]).astype(jnp.bfloat16)
    flat_table = page_table[0, 0].reshape(-1)
    own_pages = jnp.take(kv_pool[:, 0], flat_table, axis=0).reshape(
        slot_count, pages_here, PAGE, width
    )
    members = (ssm_state, conv_x, conv_bc, own_pages)
    members = migrate(members, sending, placing)
    served = lax.dynamic_index_in_dim(layout, row_index, 0, keepdims=False)
    lengths_here = jnp.take(cache_lengths, served)
    results, partials, fresh_parts, gated = serve_rows(
        projected,
        members[0],
        members[1],
        members[2],
        members[3],
        lengths_here,
        conv_weight_x,
        conv_weight_bc,
        dt_bias,
        a_log,
        d_skip,
        col_index,
        col_count,
    )
    merged_peak, merged_total, merged_sum = merged(partials, "cols", combine)
    queries, key_new, value_new = fresh_parts
    score_scale = HD ** (-0.5)
    own_score = (
        jnp.einsum("skgd,skd->skg", queries, key_new, preferred_element_type=jnp.float32)
        * score_scale
    )
    joint_peak = jnp.maximum(merged_peak, own_score)
    cache_scale = jnp.exp(merged_peak - joint_peak)
    own_weight = jnp.exp(own_score - joint_peak)
    weighted = (
        merged_sum * cache_scale[..., None]
        + own_weight[..., None] * value_new.astype(jnp.float32)[:, :, None, :]
    )
    attended = (
        (weighted / (merged_total * cache_scale + own_weight)[..., None])
        .reshape(slot_count, QH * HD)
        .astype(jnp.bfloat16)
    )
    share = QH * HD // col_count
    attn_here = lax.dynamic_slice_in_dim(attended, col_index * share, share, 1)
    out_terms = jnp.dot(gated, weight_ssm_out, preferred_element_type=jnp.float32) + jnp.dot(
        attn_here, weight_attn_out, preferred_element_type=jnp.float32
    )
    mixed = lax.psum_scatter(out_terms, "cols", scatter_dimension=1, tiled=True).astype(
        jnp.bfloat16
    )
    state_next, conv_x_next, conv_bc_next, pages_next = results
    owner = (
        jnp.zeros(flat_table.shape, jnp.int32)
        .at[flat_table]
        .set(jnp.arange(flat_table.shape[0], dtype=jnp.int32))
    )
    pool_next = jnp.take(pages_next.reshape(-1, PAGE, width), owner, axis=0)[:, None]
    return (mixed, state_next, conv_x_next, conv_bc_next, pool_next)


def solution(mesh):
    in_specs = (
        P(None, "rows"),
        P(),
        P(),
        P(),
        P(),
        P("rows", "cols", None, None),
        P("rows", "cols", None, None),
        P("rows", "cols", None, None),
        P("rows", None, "cols"),
        P("rows", None, None),
        P("rows"),
        P("rows", "cols"),
        P("rows", "cols"),
        P("rows", "cols"),
        P("rows", None),
        P("rows", None),
        P(None, "cols"),
        P(),
        P("cols"),
        P("cols"),
        P("cols"),
        P("cols", None),
        P("cols", None),
    )
    out_specs = (
        P("rows", "cols"),
        P("rows", "cols", None, None),
        P("rows", None, "cols"),
        P("rows", None, None),
        P("rows", "cols", None, None),
    )
    return jax.shard_map(local, mesh=mesh, in_specs=in_specs, out_specs=out_specs, check_vma=False)
```

profile of v0, /device:TPU:6, one launch (start us, length us, event | category | flops | bytes accessed | tf_op | source)
XLA Modules:
  0.0 589.9 jit_solution(16574519463339563221)
XLA Ops:
  13.8 2.9 scatter_custom_fusion
  16.7 3.1 gather_fusion
  24.3 79.0 %fusion = f32[16,2306]{1,0:T(8,128)S(1)} fusion(f32[416,2306]{1,0:T(8,128)} %fusion.18), kind=kCustom, calls=%all-reduce-scatter | all-reduce-scatter fusion | flops 1180673 | bytes 3986816
  103.4 7.0 %collective-permute-start.4 = (f32[16,2306]{1,0:T(8,128)S(1)}, f32[16,2306]{1,0:T(8,128)S(1)}, u32[]{:S(2)}, u32[]{:S(2)}) collective-permute-start(f32[16,2306]{1,0:T(8,128)S(1)} %fusion), channel_id=1, source_target_pairs={{0,80},{16,96},{32,112},{48,128},{64,144},{80,160},{96,176},{112,1... | collective-permute-start | bytes 442760
  110.4 16.5 %collective-permute-start.3 = (f32[16,2306]{1,0:T(8,128)S(1)}, f32[16,2306]{1,0:T(8,128)S(1)}, u32[]{:S(2)}, u32[]{:S(2)}) collective-permute-start(f32[16,2306]{1,0:T(8,128)S(1)} %fusion), channel_id=1, source_target_pairs={{0,64},{16,80},{32,96},{48,112},{64,128},{80,144},{96,160},{112,17... | collective-permute-start | bytes 442760
  128.8 7.1 %collective-permute-start.1 = (f32[16,2306]{1,0:T(8,128)S(1)}, f32[16,2306]{1,0:T(8,128)}, u32[]{:S(2)}, u32[]{:S(2)}) collective-permute-start(f32[16,2306]{1,0:T(8,128)S(1)} %fusion), channel_id=1, source_target_pairs={{0,32},{16,48},{32,64},{48,80},{64,96},{80,112},{96,128},{112,144}... | collective-permute-start | bytes 442760
  140.2 7.4 %all-to-all-start.1 = ((bf16[32,3,128]{2,1,0:T(4,128)(2,1)}), bf16[32,3,128]{2,1,0:T(4,128)(2,1)S(1)}, u32[]{:S(2)}, u32[]{:S(2)}) async-start(bf16[32,3,128]{2,1,0:T(4,128)(2,1)} %copy.177), calls=%async_computation.1 | async-start | bytes 65536 | tf_op jit(solution)/shard_map/all_to_all | solution.py:70
  153.3 3.2 broadcast_select_fusion
  159.2 9.9 %all-to-all-start.2 = ((bf16[32,3,512]{2,1,0:T(4,128)(2,1)}), bf16[32,3,512]{2,1,0:T(4,128)(2,1)S(1)}, u32[]{:S(2)}, u32[]{:S(2)}) async-start(bf16[32,3,512]{2,1,0:T(4,128)(2,1)} %copy.180), calls=%async_computation.2 | async-start | bytes 262144 | tf_op jit(solution)/shard_map/all_to_all | solution.py:73
  169.2 8.9 %all-to-all-done.2 = bf16[32,3,512]{2,1,0:T(4,128)(2,1)S(1)} async-done(((bf16[32,3,512]{2,1,0:T(4,128)(2,1)}), bf16[32,3,512]{2,1,0:T(4,128)(2,1)S(1)}, u32[]{:S(2)}, u32[]{:S(2)}) %all-to-all-start.2) | async-done | bytes 98336 | tf_op jit(solution)/shard_map/all_to_all | solution.py:73
  178.0 6.5 %all-to-all-start.3 = ((bf16[32,2,32,512]{3,2,1,0:T(8,128)(2,1)}), bf16[32,2,32,512]{3,2,1,0:T(8,128)(2,1)}, u32[]{:S(2)}, u32[]{:S(2)}) async-start(bf16[32,2,32,512]{3,2,1,0:T(8,128)(2,1)} %broadcast_select_fusion), calls=%async_computation.3 | async-start | bytes 4194304 | tf_op jit(solution)/shard_map/all_to_all | solution.py:76
  188.4 93.8 %all-reduce.1 = f32[416]{0:T(512)S(1)} all-reduce(f32[416]{0:T(512)S(1)} %fusion.16), channel_id=6, replica_groups=mesh['rows'=32,'cols'=16] {'rows'}, use_global_device_ids=true, to_apply=%region_9.10.clone | all-reduce | flops 416 | bytes 3328
  282.1 3.2 broadcast_select_fusion.1
  287.5 4.4 collective-permute-start
  292.1 3.7 collective-permute-done
  295.8 11.7 %concatenate.33 = f32[109,2306]{1,0:T(8,128)} concatenate(f32[13,2306]{1,0:T(8,128)} %collective-permute-done.5, f32[16,2306]{1,0:T(8,128)S(1)} %collective-permute-done.4, f32[16,2306]{1,0:T(8,128)S(1)} %collective-permute-done.3, f32[16,2306]{1,0:T(8,128)S(1)} %collective-permute-done.2, f32[16,2306]{1,0:T(8,128)} %collective-permute-done.1, f32[16,2306]{1,0:T(8,128)} %collective-permute-done, ...), dimensions={0} | concatenate | bytes 2010832
  314.7 25.4 %all-to-all-start = ((bf16[32,2,64,256]{3,2,1,0:T(8,128)(2,1)}), bf16[32,2,64,256]{3,2,1,0:T(8,128)(2,1)}, u32[]{:S(2)}, u32[]{:S(2)}) async-start(bf16[32,2,64,256]{3,2,1,0:T(8,128)(2,1)} %broadcast_select_fusion.1), calls=%async_computation | async-start | bytes 4194304 | tf_op jit(solution)/shard_map/all_to_all | solution.py:67
  340.2 3.5 pad_maximum_fusion.1
  346.9 62.7 %all-gather = f32[208,2,4]{2,1,0:T(2,128)S(1)} all-gather(f32[13,2,4]{2,1,0:T(2,128)S(1)} %get-tuple-element.300), channel_id=2, replica_groups=mesh['rows'=32,'cols'=16] {'cols'}, dimensions={0}, use_global_device_ids=true | all-gather | bytes 7072 | tf_op jit(solution)/shard_map/all_gather | solution.py:21
  410.6 30.8 %all-gather.1 = f32[208,2,4]{2,1,0:T(2,128)S(1)} all-gather(f32[13,2,4]{2,1,0:T(2,128)S(1)} %fusion.25), channel_id=3, replica_groups=mesh['rows'=32,'cols'=16] {'cols'}, dimensions={0}, use_global_device_ids=true | all-gather | bytes 7072 | tf_op jit(solution)/shard_map/all_gather | solution.py:21
  443.3 36.5 %all-gather.2 = f32[208,2,4,128]{3,2,1,0:T(4,128)S(1)} all-gather(f32[13,2,4,128]{3,2,1,0:T(4,128)S(1)} %fusion.10), channel_id=4, replica_groups=mesh['rows'=32,'cols'=16] {'cols'}, dimensions={0}, use_global_device_ids=true | all-gather | bytes 905216 | tf_op jit(solution)/shard_map/all_gather | solution.py:21
  483.5 17.1 %while.19 = (s32[]{:T(128)}, f32[13,2,4]{0,2,1:T(4,128)S(1)}, f32[13,2,4]{0,2,1:T(4,128)S(1)}, f32[13,2,4,128]{3,2,1,0:T(4,128)S(1)}, f32[16,13,2,4]{1,3,2,0:T(4...) while((s32[]{:T(128)}, f32[13,2,4]{0,2,1:T(4,128)S(1)}, ...), condition=%wide.region_16.18_spmd, body=%wide.region_15.17_spmd.sunk | while | flops 40565 | bytes 165719 | solution.py:27
  502.5 3.5 pad_maximum_fusion
  515.4 66.3 %reduce-scatter.4.cloned.1.call-done = f32[13,128]{1,0:T(8,128)} async-done(((f32[13,2048]{1,0:T(8,128)}), f32[13,128]{1,0:T(8,128)}) %reduce-scatter.4.cloned.1.call-update) | async-done | bytes 6672 | tf_op jit(solution)/shard_map/reduce_scatter | solution.py:287
  (282 shorter events, 76.6 us)
Async XLA Ops:
  7.2 143.3 %copy-start = (bf16[26,1,32,512]{3,2,1,0:T(8,128)(2,1)S(1)}, bf16[26,1,32,512]{3,2,1,0:T(8,128)(2,1)}, u32[]{:S(2)}) copy-start(bf16[26,1,32,512]{3,2,1,0:T(8,128)(2,1)} %param.33) | copy-start | bytes 2555908
  7.2 14.2 %copy-start.20 = (bf16[64,128]{1,0:T(8,128)(2,1)S(1)}, bf16[64,128]{1,0:T(8,128)(2,1)}, u32[]{:S(2)}) copy-start(bf16[64,128]{1,0:T(8,128)(2,1)} %param.38) | copy-start | bytes 49156
  24.3 114.2 %copy-start.15 = (s32[32,4]{0,1:T(4,128)S(1)}, s32[32,4]{0,1:T(4,128)}, u32[]{:S(2)}) copy-start(s32[32,4]{0,1:T(4,128)} %param.30) | copy-start | bytes 1540
  24.3 114.2 %copy-start.18 = (s32[32,4]{0,1:T(4,128)S(1)}, s32[32,4]{0,1:T(4,128)}, u32[]{:S(2)}) copy-start(s32[32,4]{0,1:T(4,128)} %param.31) | copy-start | bytes 1540
  24.3 114.5 %copy-start.4 = (bf16[13,3,128]{2,0,1:T(8,128)(2,1)S(1)}, bf16[13,3,128]{2,0,1:T(8,128)(2,1)}, u32[]{:S(2)}) copy-start(bf16[13,3,128]{2,0,1:T(8,128)(2,1)} %param.35) | copy-start | bytes 29956
  24.3 123.7 %copy-start.27 = (s32[1,1,13,2]{2,3,1,0:T(2,128)S(1)}, s32[1,1,13,2]{2,3,1,0:T(2,128)}, u32[]{:S(2)}) copy-start(s32[1,1,13,2]{2,3,1,0:T(2,128)} %param.32) | copy-start | bytes 316
  24.3 125.4 %copy-start.1 = (s32[416]{0:T(512)S(1)}, s32[416]{0:T(512)}, u32[]{:S(2)}) copy-start(s32[416]{0:T(512)} %param.29) | copy-start | bytes 4996
  103.4 188.7 %collective-permute-start.4 = (f32[16,2306]{1,0:T(8,128)S(1)}, f32[16,2306]{1,0:T(8,128)S(1)}, u32[]{:S(2)}, u32[]{:S(2)}) collective-permute-start(f32[16,2306]{1,0:T(8,128)S(1)} %fusion), channel_id=1, source_target_pairs={{0,80},{16,96},{32,112},{48,128},{64,144},{80,160},{96,176},{112,1... | collective-permute-start | bytes 442760
  110.4 181.7 %collective-permute-start.3 = (f32[16,2306]{1,0:T(8,128)S(1)}, f32[16,2306]{1,0:T(8,128)S(1)}, u32[]{:S(2)}, u32[]{:S(2)}) collective-permute-start(f32[16,2306]{1,0:T(8,128)S(1)} %fusion), channel_id=1, source_target_pairs={{0,64},{16,80},{32,96},{48,112},{64,128},{80,144},{96,160},{112,17... | collective-permute-start | bytes 442760
  126.8 165.2 %collective-permute-start.2 = (f32[16,2306]{1,0:T(8,128)S(1)}, f32[16,2306]{1,0:T(8,128)S(1)}, u32[]{:S(2)}, u32[]{:S(2)}) collective-permute-start(f32[16,2306]{1,0:T(8,128)S(1)} %fusion), channel_id=1, source_target_pairs={{0,48},{16,64},{32,80},{48,96},{64,112},{80,128},{96,144},{112,160... | collective-permute-start | bytes 442760
  128.8 163.3 %collective-permute-start.1 = (f32[16,2306]{1,0:T(8,128)S(1)}, f32[16,2306]{1,0:T(8,128)}, u32[]{:S(2)}, u32[]{:S(2)}) collective-permute-start(f32[16,2306]{1,0:T(8,128)S(1)} %fusion), channel_id=1, source_target_pairs={{0,32},{16,48},{32,64},{48,80},{64,96},{80,112},{96,128},{112,144}... | collective-permute-start | bytes 442760
  136.6 151.0 %collective-permute-start.5 = (f32[13,2306]{1,0:T(8,128)}, f32[13,2306]{1,0:T(8,128)}, u32[]{:S(2)}, u32[]{:S(2)}) collective-permute-start(f32[13,2306]{1,0:T(8,128)} %slice.116), channel_id=1, source_target_pairs={{0,96},{16,112},{32,128},{48,144},{64,160},{80,176},{96,192},{112,... | collective-permute-start | bytes 359744
  140.2 19.0 %all-to-all-start.1 = ((bf16[32,3,128]{2,1,0:T(4,128)(2,1)}), bf16[32,3,128]{2,1,0:T(4,128)(2,1)S(1)}, u32[]{:S(2)}, u32[]{:S(2)}) async-start(bf16[32,3,128]{2,1,0:T(4,128)(2,1)} %copy.177), calls=%async_computation.1 | async-start | bytes 65536 | tf_op jit(solution)/shard_map/all_to_all | solution.py:70
  150.5 195.6 %copy-start.16 = (pred[13]{0:T(512)(128)(4,1)}, pred[13]{0:T(512)(128)(4,1)S(1)}, u32[]{:S(2)}) copy-start(pred[13]{0:T(512)(128)(4,1)S(1)} %get-tuple-element.297) | copy-start | bytes 43
  153.3 15.8 %copy-start.33 = (f32[2]{0:T(128)S(1)}, f32[2]{0:T(128)}, u32[]{:S(2)}) copy-start(f32[2]{0:T(128)} %param.46) | copy-start | bytes 28
  157.5 252.9 %copy-start.24 = (pred[13,64]{1,0:T(8,128)(4,1)}, pred[13,64]{1,0:T(8,128)(4,1)S(1)}, u32[]{:S(2)}) copy-start(pred[13,64]{1,0:T(8,128)(4,1)S(1)} %broadcast_compare_fusion) | copy-start | bytes 2500
  158.5 185.1 %copy-start.22 = (s32[1024]{0:T(1024)}, s32[1024]{0:T(1024)S(1)}, u32[]{:S(2)}) copy-start(s32[1024]{0:T(1024)S(1)} %pad_clamp_fusion.3) | copy-start | bytes 12292
  159.2 18.8 %all-to-all-start.2 = ((bf16[32,3,512]{2,1,0:T(4,128)(2,1)}), bf16[32,3,512]{2,1,0:T(4,128)(2,1)S(1)}, u32[]{:S(2)}, u32[]{:S(2)}) async-start(bf16[32,3,512]{2,1,0:T(4,128)(2,1)} %copy.180), calls=%async_computation.2 | async-start | bytes 262144 | tf_op jit(solution)/shard_map/all_to_all | solution.py:73
  169.1 15.9 %copy-start.3 = (bf16[13,2,64,256]{3,2,1,0:T(8,128)(2,1)S(1)}, bf16[13,2,64,256]{3,2,1,0:T(8,128)(2,1)}, u32[]{:S(2)}) copy-start(bf16[13,2,64,256]{3,2,1,0:T(8,128)(2,1)} %param.34) | copy-start | bytes 2555908
  178.0 136.7 %all-to-all-start.3 = ((bf16[32,2,32,512]{3,2,1,0:T(8,128)(2,1)}), bf16[32,2,32,512]{3,2,1,0:T(8,128)(2,1)}, u32[]{:S(2)}, u32[]{:S(2)}) async-start(bf16[32,2,32,512]{3,2,1,0:T(8,128)(2,1)} %broadcast_select_fusion), calls=%async_computation.3 | async-start | bytes 4194304 | tf_op jit(solution)/shard_map/all_to_all | solution.py:76
  285.4 25.7 %copy-start.31 = (f32[2]{0:T(128)S(1)}, f32[2]{0:T(128)}, u32[]{:S(2)}) copy-start(f32[2]{0:T(128)} %param.45) | copy-start | bytes 28
  287.5 8.2 %collective-permute-start = (f32[16,2306]{1,0:T(8,128)S(1)}, f32[16,2306]{1,0:T(8,128)}, u32[]{:S(2)}, u32[]{:S(2)}) collective-permute-start(f32[16,2306]{1,0:T(8,128)S(1)} %fusion), channel_id=1, source_target_pairs={{0,16},{16,32},{32,48},{48,64},{64,80},{80,96},{96,112},{112,128},... | collective-permute-start | bytes 442760
  314.7 187.8 %all-to-all-start = ((bf16[32,2,64,256]{3,2,1,0:T(8,128)(2,1)}), bf16[32,2,64,256]{3,2,1,0:T(8,128)(2,1)}, u32[]{:S(2)}, u32[]{:S(2)}) async-start(bf16[32,2,64,256]{3,2,1,0:T(8,128)(2,1)} %broadcast_select_fusion.1), calls=%async_computation | async-start | bytes 4194304 | tf_op jit(solution)/shard_map/all_to_all | solution.py:67
  340.1 241.6 %reduce-scatter.4.cloned.1.call-start = ((), (), s32[]{:S(2)}) async-start(), calls=%async_computation.5 | async-start | bytes 139264 | tf_op jit(solution)/shard_map/reduce_scatter | solution.py:287
  (21 other events, 104.4 us)
Sparse Core Ops, SparseCore 0:
  513.5 68.1 reduce-scatter.3
where the time goes:
time: 592 us; the launch traced here: 590 us
  blocking collectives  303 us (51%)
  starting transfers between devices  87.9 us (15%)
  waiting for transfers between devices  78.9 us (13%)
  local copies, waits for them, and re-layouts  52 us (9%)
  other arithmetic  44.2 us (7%)
  between operations  16.3 us (3%)
  matrix products  7.55 us (1%)
    unnamed x2, blocking collectives  173 us
    all_gather x3, blocking collectives, merged(): everything = jax.tree.map(lambda part: lax.all_gather(part, axis), value)  130 us
    reduce_scatter x1, waiting for transfers between devices, local(): lax.psum_scatter(out_terms, 'cols', scatter_dimension=1, tiled=True)  66.3 us
    unnamed x6, starting transfers between devices  38.8 us
    all_to_all x1, starting transfers between devices, migrate(): lax.all_to_all(jnp.take(state_part, sending, axis=0), 'rows', split_axis=...  25.4 us
    unnamed x79, local copies, waits for them, and re-layouts  17.8 us
  transfers between devices with their start and end apart: 11, of which 3 were waited for; matrix products, arithmetic and copies ran while one was open for 12% of the time, Pallas kernels for 0%

commit v1 on v0

v1 whole, which is shorter than its diff:
```python
import jax
import jax.numpy as jnp
from jax import lax
from jax.experimental import pallas as pl
from jax.experimental.pallas import tpu as pltpu
from jax.sharding import PartitionSpec as P

D = 2048
HP = 64
NS = 256
HD = 128
PAGE = 32
SLOTS = 13
ROWS = 32
COLS = 16
MOVES = 4
EPSILON = 1e-05
FLOOR = -1e30
F32 = jnp.float32
BF16 = jnp.bfloat16
I32 = jnp.int32
MESH = pl.DeviceIdType.MESH


def nt(a, b):
    return lax.dot_general(a, b, (((1,), (1,)), ((), ())), preferred_element_type=F32)


def nn(a, b):
    return jnp.dot(a, b, preferred_element_type=F32)


def silu(v):
    return v / (1.0 + jnp.exp(-v))


def tables_kernel(ms_ref, mt_ref, pt_ref, layout_ref, source_ref, owner_ref):
    row = lax.axis_index("rows")
    for j in range(2 * SLOTS):
        owner_ref[pt_ref[j]] = j
    lane = lax.broadcasted_iota(I32, (128, 128), 1)
    sub = lax.broadcasted_iota(I32, (128, 128), 0)
    eye = lane == sub
    lane_f = lane.astype(F32)
    sub_f = sub.astype(F32)
    ms = jnp.broadcast_to(ms_ref[...].astype(F32), (128, 128))
    mt = jnp.broadcast_to(mt_ref[...].astype(F32), (128, 128))

    def column(v):
        return jnp.sum(jnp.where(eye, v, 0.0), axis=1, keepdims=True)

    def down(v):
        return jnp.sum(v, axis=0, keepdims=True)

    mt_col = column(mt)
    ms_col = column(ms)
    rank = down(jnp.where((mt_col == mt) & (sub < lane), 1.0, 0.0))
    place = 4.0 * mt + jnp.broadcast_to(rank, (128, 128))
    slot_there = down(jnp.where(sub_f == place, jnp.broadcast_to(ms_col, (128, 128)), 0.0))
    place_col = column(place)
    kept_at = (((row - (sub >> 2)) & (ROWS - 1)) * 8 + (sub & 3)).astype(F32)
    source_ref[...] = down(jnp.where(place_col == lane_f, kept_at, 0.0)).astype(I32)
    lane1 = lax.broadcasted_iota(I32, (1, 128), 1)
    goes = 16.0 * mt_ref[...].astype(F32) + slot_there
    left = ((lane1 >> 2) * 16).astype(F32) + ms_ref[...].astype(F32)
    request = ((lane1 >> 2) * SLOTS).astype(F32) + ms_ref[...].astype(F32)
    q = lax.broadcasted_iota(I32, (512, 128), 0)
    q_f = q.astype(F32)
    arrived = jnp.sum(jnp.where(q_f == goes, request, 0.0), axis=1, keepdims=True)
    vacated = jnp.sum(jnp.where(q_f == left, 1.0, 0.0), axis=1, keepdims=True)
    q1 = lax.broadcasted_iota(I32, (512, 1), 0)
    s1 = q1 & 15
    stays = (q1 >> 4) * SLOTS + s1
    layout = jnp.where(vacated > 0.5, arrived.astype(I32), stays)
    layout_ref[...] = jnp.where(s1 < SLOTS, layout, -1)


def mixer_kernel(
    ms, mt, lengths, source, pt, owner, dtb, alog, dskip,
    layout, arrival, tokens, gain, wz, wx, wdt, wbc, wqkv, convp, cwx, cwbc, wssm, wattn,
    pool, state,
    kv_out, state_out, mixed_out, cx_out, cbc_out,
    send1, recv1, send2, recv2, pcomb, scomb, kvn, stn, ccomb, cbuf,
    send_s, recv_s, qbuf, fresh, obuf, pbuf, tbuf, send_a, recv_a, send_o, recv_o,
    s1_sem, r1_sem, s2_sem, r2_sem, ss_sem, rs_sem, sa_sem, ra_sem, so_sem, ro_sem,
    in_sem, out_sem,
):
    row = lax.axis_index("rows")
    col = lax.axis_index("cols")

    pool_copy = pltpu.make_async_copy(pool, pcomb.at[pl.ds(0, 26)], in_sem.at[0])
    state_copy = pltpu.make_async_copy(state, scomb.at[pl.ds(0, SLOTS)], in_sem.at[1])
    pool_copy.start()
    state_copy.start()

    barrier = pltpu.get_barrier_semaphore()

    def greet_rows(d, carry):
        pl.semaphore_signal(barrier, inc=1, device_id=((row + d) & (ROWS - 1), col), device_id_type=MESH)
        return carry

    def greet_cols(d, carry):
        pl.semaphore_signal(barrier, inc=1, device_id=(row, (col + d) & (COLS - 1)), device_id_type=MESH)
        return carry

    lax.fori_loop(1, ROWS, greet_rows, 0)
    lax.fori_loop(1, COLS, greet_cols, 0)

    onehot = jnp.where(layout[...] == arrival[...], 1.0, 0.0).astype(BF16)
    picked = nn(onehot, tokens[...])
    scaled = (picked * gain[...].astype(F32)).astype(BF16)
    squares = jnp.square(picked)
    squares_hi = squares.astype(BF16)
    squares_lo = (squares - squares_hi.astype(F32)).astype(BF16)
    last = (lax.broadcasted_iota(I32, (16, 64), 0) == 15).astype(F32).astype(BF16)
    extra = nt(wdt[...], scaled) + nt(last, squares_hi) + nt(last, squares_lo)
    bc_at = pl.multiple_of(jnp.minimum(col, 3) * 128, 128)
    qkv_at = pl.multiple_of(jnp.maximum(col - 4, 0) * 128, 128)
    shared = jnp.where(
        col < 4, wbc[:, pl.ds(bc_at, 128)].astype(F32), wqkv[:, pl.ds(qkv_at, 128)].astype(F32)
    ).astype(BF16)
    part_z = nn(scaled, wz[...]).reshape(4, 8, 16, 128)
    for u in range(4):
        tile = part_z[u] + extra[:, 128 * u : 128 * (u + 1)][None]
        send1[8 * u : 8 * (u + 1), 5] = tile.astype(BF16)
    send1[:, 6] = nn(scaled, wx[...]).reshape(ROWS, 16, 128).astype(BF16)
    send1[:, 7] = nn(scaled, shared).reshape(ROWS, 16, 128).astype(BF16)

    slots = [ms[MOVES * row + m] for m in range(MOVES)]
    targets = [mt[MOVES * row + m] for m in range(MOVES)]

    def conv_tile(t, carry):
        at = slots[0]
        for m in range(1, MOVES):
            at = jnp.where(targets[m] == t, slots[m], at)
        send1[t, 4] = convp[at]
        return carry

    lax.fori_loop(0, ROWS, conv_tile, 0)
    pool_copy.wait()
    state_copy.wait()

    def cut(m, carry):
        slot = ms[MOVES * row + m]
        for p in range(16):
            r, l = 16 * (p // 2), 128 * (p % 2)
            send1[p, m] = scomb[slot, r : r + 16, l : l + 128]
        for page in range(2):
            g = pt[2 * slot + page]
            for i in range(8):
                r, l = 16 * (i // 4), 128 * (i % 4)
                send1[16 + 8 * page + i, m] = pcomb[g, r : r + 16, l : l + 128]
        return carry

    lax.fori_loop(0, MOVES, cut, 0)

    pl.semaphore_wait(barrier, ROWS + COLS - 2)

    def hop1(d, carry):
        to = (row + d) & (ROWS - 1)
        pltpu.make_async_remote_copy(
            send1.at[to], recv1.at[pl.ds(8 * d, 8)], s1_sem, r1_sem, device_id=(to, col), device_id_type=MESH
        ).start()
        return carry

    lax.fori_loop(1, ROWS, hop1, 0)
    recv1[0:8] = send1[row]
    away1 = recv1.at[pl.ds(8, 8 * (ROWS - 1))]
    pltpu.make_async_copy(away1, away1, r1_sem).wait()

    def pick(t, carry):
        for k in range(MOVES):
            send2[t, k] = recv1[source[MOVES * t + k]]
        return carry

    lax.fori_loop(0, ROWS, pick, 0)

    def hop2(d, carry):
        to = (row + d) & (ROWS - 1)
        pltpu.make_async_remote_copy(
            send2.at[to], recv2.at[d], s2_sem, r2_sem, device_id=(to, col), device_id_type=MESH
        ).start()
        return carry

    lax.fori_loop(1, ROWS, hop2, 0)
    recv2[0] = send2[row]

    def add(d, sums):
        return tuple(sums[j] + recv1[8 * d + 5 + j].astype(F32) for j in range(3))

    zero = jnp.zeros((16, 128), F32)
    sum_z, sum_x, sum_s = lax.fori_loop(0, ROWS, add, (zero, zero, zero))
    lane = lax.broadcasted_iota(I32, (16, 128), 1)
    sub = lax.broadcasted_iota(I32, (16, 128), 0)
    low = lane < HP
    mine = lane == sub + 16 * (row & 7)

    def as_column(k):
        return jnp.sum(jnp.where(mine, jnp.broadcast_to(sum_z[k : k + 1], (16, 128)), 0.0), axis=1, keepdims=True)

    root = jnp.sqrt(as_column(15) / D + EPSILON)
    gate_in = jnp.where(sub < SLOTS, sum_z / root, 0.0).astype(BF16).astype(F32)
    value_in = (sum_x / root).astype(BF16)
    step_in = jnp.where(low, as_column(13) / root, as_column(14) / root).astype(BF16).astype(F32)
    send_s[...] = (sum_s / root).astype(BF16)

    def share(d, carry):
        to = (col + d) & (COLS - 1)
        pltpu.make_async_remote_copy(
            send_s, recv_s.at[d], ss_sem, rs_sem, device_id=(row, to), device_id_type=MESH
        ).start()
        return carry

    lax.fori_loop(1, COLS, share, 0)
    recv_s[0] = send_s[...]

    ccomb[0:SLOTS] = convp[...]
    for k in range(MOVES):
        ccomb[SLOTS + k] = recv1[((source[MOVES * row + k] >> 3) << 3) + 4]
    places = []
    for s in range(SLOTS):
        at = jnp.int32(s)
        for k in range(MOVES):
            at = jnp.where(slots[k] == s, SLOTS + k, at)
        places.append(at)
        cbuf[:, s, :] = ccomb[at].astype(F32)
    for s in range(SLOTS, 16):
        cbuf[:, s, :] = zero

    taps_x = cwx[...].astype(F32)
    taps_bc = cwbc[...].astype(F32)
    conv = value_in.astype(F32) * taps_x[3:4]
    for k in range(3):
        conv = conv + cbuf[k] * taps_x[k : k + 1]
    value_act = silu(conv)
    cx_out[0] = cbuf[1].astype(BF16)
    cx_out[1] = cbuf[2].astype(BF16)
    cx_out[2] = value_in
    head_lanes = lambda ref: jnp.where(low, ref[0], ref[1])
    raw_step = step_in + head_lanes(dtb)
    step = jnp.maximum(raw_step, 0.0) + jnp.log1p(jnp.exp(-jnp.abs(raw_step)))
    decay = jnp.exp(-jnp.exp(head_lanes(alog)) * step)
    grown = step * value_act

    away_s = recv_s.at[pl.ds(1, COLS - 1)]
    pltpu.make_async_copy(away_s, away_s, rs_sem).wait()

    def chunk(c):
        return recv_s[(col - c) & (COLS - 1)]

    act = []
    for c in range(4):
        new = chunk(c)
        lanes = slice(128 * c, 128 * (c + 1))
        conv = new.astype(F32) * taps_bc[3:4, lanes]
        for k in range(3):
            conv = conv + cbuf[3 + 4 * k + c] * taps_bc[k : k + 1, lanes]
        act.append(silu(conv).astype(BF16))
        cbc_out[0, :, lanes] = cbuf[3 + 4 + c].astype(BF16)
        cbc_out[1, :, lanes] = cbuf[3 + 8 + c].astype(BF16)
        cbc_out[2, :, lanes] = new
    b_in = jnp.concatenate(act[:2], axis=1)
    c_out = jnp.concatenate(act[2:], axis=1)
    qbuf[...] = jnp.zeros_like(qbuf)
    for h in range(8):
        lanes = slice(128 * (h // 4), 128 * (h // 4 + 1))
        qbuf[:, h, lanes] = chunk(4 + h).astype(F32)
    for j in range(4):
        fresh[:, 0, 128 * j : 128 * (j + 1)] = chunk(12 + j).astype(F32)

    away2 = recv2.at[pl.ds(1, ROWS - 1)]
    pltpu.make_async_copy(away2, away2, r2_sem).wait()

    def paste(k, carry):
        for p in range(16):
            r, l = 16 * (p // 2), 128 * (p % 2)
            scomb[SLOTS + k, r : r + 16, l : l + 128] = recv2[(row - p) & (ROWS - 1), k]
        for p in range(16):
            i = p % 8
            r, l = 16 * (i // 4), 128 * (i % 4)
            pcomb[26 + 2 * k + p // 8, r : r + 16, l : l + 128] = recv2[(row - 16 - p) & (ROWS - 1), k]
        return carry

    lax.fori_loop(0, MOVES, paste, 0)

    def length_of(s):
        request = row * SLOTS + s
        for k in range(MOVES):
            code = source[MOVES * row + k]
            at = (row - (code >> 3)) & (ROWS - 1)
            request = jnp.where(slots[k] == s, at * SLOTS + ms[MOVES * at + (code & 3)], request)
        return lengths[request]

    line = lax.broadcasted_iota(I32, (PAGE, 512), 0)

    def page(g, carry):
        entry = owner[g]
        s, half = entry >> 1, entry & 1
        at = g
        for k in range(MOVES):
            at = jnp.where(slots[k] == s, 26 + 2 * k + half, at)
        length = length_of(s)
        logical = length >> 5
        here = ((logical & (COLS - 1)) == col) & ((logical >> 4) == half)
        offset = jnp.where(here, length & (PAGE - 1), -1)
        kvn[g] = jnp.where(line == offset, fresh[s].astype(F32), pcomb[at].astype(F32)).astype(BF16)
        return carry

    lax.fori_loop(0, 26, page, 0)
    kv_copy = pltpu.make_async_copy(kvn, kv_out, out_sem.at[0])
    kv_copy.start()

    for ref in (obuf, pbuf, tbuf):
        ref[...] = jnp.zeros_like(ref)
    token = lax.broadcasted_iota(I32, (8, 64), 1)
    position = (token >> 5) * (COLS * PAGE) + col * PAGE + (token & (PAGE - 1))
    head = lax.broadcasted_iota(I32, (8, 128), 0)
    for s in range(SLOTS):
        both = jnp.concatenate([kvn[pt[2 * s]], kvn[pt[2 * s + 1]]], axis=0)
        scores = nt(qbuf[s].astype(BF16), both[:, :256]) * (HD**-0.5)
        live = position <= length_of(s)
        peak = jnp.max(jnp.where(live, scores, FLOOR), axis=1, keepdims=True)
        weights = jnp.where(live, jnp.exp(scores - peak), 0.0)
        summed = nn(weights.astype(BF16), both[:, 256:])
        obuf[:, s, :] = jnp.where(head < 4, summed[:, :128], summed[:, 128:])
        pbuf[:, s, :] = jnp.broadcast_to(peak, (8, 128))
        tbuf[:, s, :] = jnp.broadcast_to(jnp.sum(weights, axis=1, keepdims=True), (8, 128))
    for h in range(8):
        stats = jnp.where(lane == HP, pbuf[h], tbuf[h])
        send_a[2 * h] = jnp.where(low, obuf[h], stats)
        send_a[2 * h + 1] = jnp.where(low, pltpu.roll(obuf[h], HP, 1), stats)

    def attend(d, carry):
        to = (col + d) & (COLS - 1)
        pltpu.make_async_remote_copy(
            send_a.at[to], recv_a.at[d], sa_sem, ra_sem, device_id=(row, to), device_id_type=MESH
        ).start()
        return carry

    lax.fori_loop(1, COLS, attend, 0)
    recv_a[0] = send_a[col]

    read = zero
    for s in range(SLOTS):
        read = jnp.where(sub == s, nt(c_out, scomb[places[s]]), read)
    b_dot_c = jnp.sum(b_in.astype(F32) * c_out.astype(F32), axis=1, keepdims=True)
    readout = decay * read + grown * b_dot_c + head_lanes(dskip) * value_act
    gated = (readout * silu(gate_in)).astype(BF16)
    out_terms = nn(gated, wssm[...])

    away_a = recv_a.at[pl.ds(1, COLS - 1)]
    pltpu.make_async_copy(away_a, away_a, ra_sem).wait()
    top = recv_a[0]
    for d in range(1, COLS):
        top = jnp.maximum(top, recv_a[d])
    top = top[:, HP : HP + 1]
    gathered = zero
    for d in range(COLS):
        part = recv_a[d]
        gathered = gathered + part * jnp.exp(part[:, HP : HP + 1] - top)
    attended = (gathered / gathered[:, HP + 1 : HP + 2]).astype(BF16)
    out_terms = out_terms + nn(attended[:, :HP], wattn[...])
    for c in range(COLS):
        send_o[c] = out_terms[:, 128 * c : 128 * (c + 1)].astype(BF16)

    def project(d, carry):
        to = (col + d) & (COLS - 1)
        pltpu.make_async_remote_copy(
            send_o.at[to], recv_o.at[d], so_sem, ro_sem, device_id=(row, to), device_id_type=MESH
        ).start()
        return carry

    lax.fori_loop(1, COLS, project, 0)
    recv_o[0] = send_o[col]

    columns = jnp.concatenate([grown, decay, jnp.zeros((96, 128), F32)], axis=0).T
    for s in range(SLOTS):
        old = scomb[places[s]].astype(F32)
        new = columns[:, 16 + s : 17 + s] * old + columns[:, s : s + 1] * b_in[s : s + 1].astype(F32)
        stn[s] = new.astype(BF16)
    state_copy_out = pltpu.make_async_copy(stn, state_out, out_sem.at[1])
    state_copy_out.start()

    away_o = recv_o.at[pl.ds(1, COLS - 1)]
    pltpu.make_async_copy(away_o, away_o, ro_sem).wait()
    mixed = zero
    for d in range(COLS):
        mixed = mixed + recv_o[d].astype(F32)
    mixed_out[...] = mixed.astype(BF16)

    sent1 = send1.at[pl.ds(0, ROWS - 1)]
    pltpu.make_async_copy(sent1, sent1, s1_sem).wait()
    sent2 = send2.at[pl.ds(0, ROWS - 1)]
    pltpu.make_async_copy(sent2, sent2, s2_sem).wait()
    for sem, ref in ((ss_sem, recv_s), (sa_sem, send_a), (so_sem, send_o)):
        sent = ref.at[pl.ds(0, COLS - 1)]
        pltpu.make_async_copy(sent, sent, sem).wait()
    kv_copy.wait()
    state_copy_out.wait()


def local(
    tokens, arrival, cache_lengths, move_slot, move_target, page_table, kv_pool, ssm_state, conv_x, conv_bc,
    norm_gain, weight_z, weight_x, weight_dt, weight_bc, weight_qkv, conv_weight_x, conv_weight_bc,
    dt_bias, a_log, d_skip, weight_ssm_out, weight_attn_out,
):
    vmem = pl.BlockSpec(memory_space=pltpu.VMEM)
    smem = pl.BlockSpec(memory_space=pltpu.SMEM)
    anywhere = pl.BlockSpec(memory_space=pl.ANY)
    shape = jax.ShapeDtypeStruct
    pt = page_table.reshape(2 * SLOTS)
    ms = move_slot.reshape(ROWS * MOVES)
    mt = move_target.reshape(ROWS * MOVES)
    layout, source, owner = pl.pallas_call(
        tables_kernel,
        out_shape=(shape((512, 1), I32), shape((1, 128), I32), shape((2 * SLOTS,), I32)),
        in_specs=[vmem, vmem, smem],
        out_specs=(vmem, vmem, smem),
        name="tables",
    )(ms.reshape(1, 128), mt.reshape(1, 128), pt)

    convp = jnp.concatenate(
        [conv_x, conv_bc.reshape(SLOTS, 12, 128), jnp.zeros((SLOTS, 1, 128), BF16)], axis=1
    )
    wdt = jnp.pad(weight_dt.T, ((13, 1), (0, 0)))
    dma = pltpu.SemaphoreType.DMA
    kv_next, state_next, mixed, cx, cbc = pl.pallas_call(
        mixer_kernel,
        out_shape=(
            shape((26, PAGE, 512), BF16),
            shape((SLOTS, 128, NS), BF16),
            shape((16, 128), BF16),
            shape((3, 16, 128), BF16),
            shape((3, 16, 512), BF16),
        ),
        in_specs=[smem] * 9 + [vmem] * 14 + [anywhere] * 2,
        out_specs=(anywhere, anywhere, vmem, vmem, vmem),
        scratch_shapes=[
            pltpu.VMEM((ROWS, 8, 16, 128), BF16),
            pltpu.VMEM((ROWS * 8, 16, 128), BF16),
            pltpu.VMEM((ROWS, MOVES, 16, 128), BF16),
            pltpu.VMEM((ROWS, MOVES, 16, 128), BF16),
            pltpu.VMEM((34, PAGE, 512), BF16),
            pltpu.VMEM((SLOTS + MOVES, 128, NS), BF16),
            pltpu.VMEM((26, PAGE, 512), BF16),
            pltpu.VMEM((SLOTS, 128, NS), BF16),
            pltpu.VMEM((SLOTS + MOVES, 16, 128), BF16),
            pltpu.VMEM((16, 16, 128), F32),
            pltpu.VMEM((16, 128), BF16),
            pltpu.VMEM((COLS, 16, 128), BF16),
            pltpu.VMEM((16, 8, 256), F32),
            pltpu.VMEM((16, 1, 512), F32),
            pltpu.VMEM((8, 16, 128), F32),
            pltpu.VMEM((8, 16, 128), F32),
            pltpu.VMEM((8, 16, 128), F32),
            pltpu.VMEM((COLS, 16, 128), F32),
            pltpu.VMEM((COLS, 16, 128), F32),
            pltpu.VMEM((COLS, 16, 128), BF16),
            pltpu.VMEM((COLS, 16, 128), BF16),
        ]
        + [dma] * 10
        + [dma((2,)), dma((2,))],
        compiler_params=pltpu.CompilerParams(
            collective_id=0, has_side_effects=True, vmem_limit_bytes=48 * 1024 * 1024
        ),
        name="mixer",
    )(
        ms, mt, cache_lengths, source.reshape(128), pt, owner, dt_bias, a_log, d_skip,
        layout, arrival.reshape(1, 416), tokens, norm_gain.reshape(1, 64), weight_z, weight_x, wdt,
        weight_bc, weight_qkv, convp, conv_weight_x, conv_weight_bc, weight_ssm_out, weight_attn_out,
        kv_pool.reshape(26, PAGE, 512), ssm_state.reshape(SLOTS, 128, NS),
    )
    return (
        mixed[:SLOTS],
        state_next.reshape(SLOTS, 2, HP, NS),
        cx.transpose(1, 0, 2)[:SLOTS],
        cbc.transpose(1, 0, 2)[:SLOTS],
        kv_next.reshape(26, 1, PAGE, 512),
    )


def solution(mesh):
    in_specs = (
        P(None, "rows"), P(), P(), P(), P(), P("rows", "cols", None, None), P("rows", "cols", None, None),
        P("rows", "cols", None, None), P("rows", None, "cols"), P("rows", None, None), P("rows"),
        P("rows", "cols"), P("rows", "cols"), P("rows", "cols"), P("rows", None), P("rows", None),
        P(None, "cols"), P(), P("cols"), P("cols"), P("cols"), P("cols", None), P("cols", None),
    )
    out_specs = (
        P("rows", "cols"),
        P("rows", "cols", None, None),
        P("rows", None, "cols"),
        P("rows", None, None),
        P("rows", "cols", None, None),
    )
    return jax.shard_map(local, mesh=mesh, in_specs=in_specs, out_specs=out_specs, check_vma=False)
```

time: 592 us -> 94.5 us (0.16)
  blocking collectives: 303 us -> 0 us
  starting transfers between devices: 87.9 us -> 0 us
  waiting for transfers between devices: 78.9 us -> 0 us
  Pallas kernels: 0 us -> 74.6 us
  other arithmetic: 44.2 us -> 0.08 us
  local copies, waits for them, and re-layouts: 52 us -> 18.4 us
  between operations: 16.3 us -> 0.85 us
  matrix products: 7.55 us -> 0 us
    unnamed x2 -> x0, blocking collectives: 173 us -> none
    all_gather x3 -> x0, blocking collectives: 130 us -> none  [merged(): everything = jax.tree.map(lambda part: lax.all_gather(part, axis), value)]
    pallas_call x0 -> x2, Pallas kernels: none -> 74.6 us  [the longest x1 72.8 us: local(): pl.pallas_call(mixer_kernel, out_shape=(shape((26, PAGE, 512), BF16), sha...]
    reduce_scatter x1 -> x0, waiting for transfers between devices: 66.3 us -> none  [local(): lax.psum_scatter(out_terms, 'cols', scatter_dimension=1, tiled=True)]
    all_to_all x4 -> x0, starting transfers between devices: 49.1 us -> none  [the longest x1 25.4 us: migrate(): lax.all_to_all(jnp.take(state_part, sending, axis=0), 'rows', split_axis=...]
    unnamed x6 -> x0, starting transfers between devices: 38.8 us -> none
    gather x13 -> x0, local copies, waits for them, and re-layouts: 18.4 us -> none  [the longest x4 6.19 us: migrate(): jnp.take(jnp.concatenate([resident_part, arrived_part], axis=0), placing,...]
    add x34 -> x0, other arithmetic: 14.7 us -> none  [the longest x15 10.8 us: combine(): joint_total = first_part[1] * first_scale + second_part[1] * second_scale]
  transfers between devices with their start and end apart: 11 -> 0, of which waited for: 3 -> 0; matrix products, arithmetic and copies ran while one was open for 12% -> 0% of each run, Pallas kernels for 0% -> 0%
where the time goes in v1:
time: 94.5 us; the launch traced here: 93.9 us
  Pallas kernels  74.6 us (79%)
  local copies, waits for them, and re-layouts  18.4 us (19%)
    pallas_call x1, Pallas kernels, local(): pl.pallas_call(mixer_kernel, out_shape=(shape((26, PAGE, 512), BF16), sha...  72.8 us
    unnamed x51, local copies, waits for them, and re-layouts  15.5 us

profile of v1, /device:TPU:6, one launch (start us, length us, event | category | flops | bytes accessed | tf_op | source)
XLA Modules:
  0.0 93.9 jit_solution(8259617412997672795)
XLA Ops:
  0.7 0.7 pad.4.wdt
  1.4 0.8 copy.41
  2.2 0.6 reshape.45.pt_ref.pt
  2.8 0.7 copy.43
  3.5 0.8 copy.37
  4.3 0.6 reshape_reshape.6.ms_ref
  5.0 0.8 copy.38
  5.8 0.6 reshape_reshape.7.mt_ref
  6.5 0.8 copy.42
  7.5 1.0 %copy.44.tokens = bf16[416,64]{1,0:T(8,128)(2,1)S(1)} copy(bf16[416,64]{0,1:T(8,128)(2,1)} %param.23) | data formatting | bytes 106496 | tf_op args[0]
  8.5 1.8 %tables.1 = (s32[512,1]{1,0:T(8,128)}, s32[1,128]{1,0:T(1,128)}, s32[26]{0:T(128)}) custom-call(s32[1,128]{1,0:T(1,128)} %reshape_reshape.6.ms_ref, s32[1,128]{1,0:T(1,128)} %reshape_reshape.7.mt_ref, s32[26]{0:T(128)} %reshape.45.pt_ref.pt), custom_call_target="tpu_custom_call" | custom-call | tf_op jit(solution)/shard_map/tables/pallas_call | solution.py:414
  11.1 1.2 %copy-done = bf16[26,1,32,512]{3,2,1,0:T(8,128)(2,1)S(1)} copy-done((bf16[26,1,32,512]{3,2,1,0:T(8,128)(2,1)S(1)}, bf16[26,1,32,512]{3,2,1,0:T(8,128)(2,1)}, u32[]{:S(2)}) %copy-start) | copy-done | bytes 851992
  12.3 1.2 %copy-done.1 = bf16[13,2,64,256]{3,2,1,0:T(8,128)(2,1)S(1)} copy-done((bf16[13,2,64,256]{3,2,1,0:T(8,128)(2,1)S(1)}, bf16[13,2,64,256]{3,2,1,0:T(8,128)(2,1)}, u32[]{:S(2)}) %copy-start.1) | copy-done | bytes 851992
  13.4 0.9 %copy-done.3 = bf16[64,2048]{1,0:T(8,128)(2,1)S(1)} copy-done((bf16[64,2048]{1,0:T(8,128)(2,1)S(1)}, bf16[64,2048]{1,0:T(8,128)(2,1)}, u32[]{:S(2)}) %copy-start.3) | copy-done | bytes 262168
  14.4 0.9 %copy-done.4 = s32[512,1]{1,0:T(8,128)S(1)} copy-done((s32[512,1]{1,0:T(8,128)S(1)}, s32[512,1]{1,0:T(8,128)}, u32[]{:S(2)}) %copy-start.4) | copy-done | bytes 2072
  15.3 0.9 copy-done.5
  16.3 0.7 copy-done.18
  16.9 0.6 copy-done.19
  17.5 72.8 %mixer.1 = (bf16[26,32,512]{2,1,0:T(8,128)(2,1)S(1)}, bf16[13,128,256]{2,1,0:T(8,128)(2,1)S(1)}, bf16[16,128]{1,0:T(8,128)(2,1)S(1)}, bf16[3,16,128]{2,1,0:T(8,128)(2,1)S(1)}, bf16[3,16,512]{2,1,0:T(8,128)(2,1)S(1)}) custom-call(s32[128]{0:T(128)S(1)} %reshape.43.ms, s32[128]{0:T(128)S(1)} %reshape.44.mt, s32[416]{0:T(512)S(1)} %copy-done.10, ...), custom_call_target="tpu_custom_call" | custom-call | tf_op jit(solution)/shard_map/mixer/pallas_call | solution.py:427
  90.3 0.6 copy.51
  90.9 0.9 copy.52
  91.8 0.6 copy.53
  92.4 0.6 copy.54
  93.0 0.9 copy.55
  (38 shorter events, 1.1 us)
Async XLA Ops:
  0.6 9.8 %copy-start.2 = (bf16[128,2048]{1,0:T(8,128)(2,1)S(1)}, bf16[128,2048]{1,0:T(8,128)(2,1)}, u32[]{:S(2)}) copy-start(bf16[128,2048]{1,0:T(8,128)(2,1)} %wssm.1) | copy-start | bytes 1572868
  7.4 3.0 %copy-start.6 = (bf16[64,512]{1,0:T(8,128)(2,1)S(1)}, bf16[64,512]{1,0:T(8,128)(2,1)}, u32[]{:S(2)}) copy-start(bf16[64,512]{1,0:T(8,128)(2,1)} %wbc.1) | copy-start | bytes 196612
  7.5 3.0 %copy-start.7 = (bf16[64,128]{1,0:T(8,128)(2,1)S(1)}, bf16[64,128]{1,0:T(8,128)(2,1)}, u32[]{:S(2)}) copy-start(bf16[64,128]{1,0:T(8,128)(2,1)} %wz.1) | copy-start | bytes 49156
  7.5 3.0 %copy-start.8 = (bf16[64,128]{1,0:T(8,128)(2,1)S(1)}, bf16[64,128]{1,0:T(8,128)(2,1)}, u32[]{:S(2)}) copy-start(bf16[64,128]{1,0:T(8,128)(2,1)} %wx.1) | copy-start | bytes 49156
  7.5 3.0 %copy-start.11 = (s32[416]{0:T(512)S(1)}, s32[416]{0:T(512)}, u32[]{:S(2)}) copy-start(s32[416]{0:T(512)} %param.24) | copy-start | bytes 4996
  7.5 3.0 %copy-start.17 = (bf16[64]{0:T(256)(128)(2,1)S(1)}, bf16[64]{0:T(256)(128)(2,1)}, u32[]{:S(2)}) copy-start(bf16[64]{0:T(256)(128)(2,1)} %param.33) | copy-start | bytes 388
  8.5 2.0 %copy-start.14 = (f32[2]{0:T(128)S(1)}, f32[2]{0:T(128)}, u32[]{:S(2)}) copy-start(f32[2]{0:T(128)} %dtb.1) | copy-start | bytes 28
  8.5 2.0 %copy-start.15 = (f32[2]{0:T(128)S(1)}, f32[2]{0:T(128)}, u32[]{:S(2)}) copy-start(f32[2]{0:T(128)} %alog.1) | copy-start | bytes 28
  8.5 2.0 %copy-start.16 = (f32[2]{0:T(128)S(1)}, f32[2]{0:T(128)}, u32[]{:S(2)}) copy-start(f32[2]{0:T(128)} %dskip.1) | copy-start | bytes 28
  10.4 0.7 copy-start.9
  10.4 0.7 copy-start.10
  10.4 0.7 copy-start.12
  10.4 0.7 copy-start.13
  11.1 1.2 %copy-start = (bf16[26,1,32,512]{3,2,1,0:T(8,128)(2,1)S(1)}, bf16[26,1,32,512]{3,2,1,0:T(8,128)(2,1)}, u32[]{:S(2)}) copy-start(bf16[26,1,32,512]{3,2,1,0:T(8,128)(2,1)} %param.29) | copy-start | bytes 2555908
  12.3 1.2 %copy-start.1 = (bf16[13,2,64,256]{3,2,1,0:T(8,128)(2,1)S(1)}, bf16[13,2,64,256]{3,2,1,0:T(8,128)(2,1)}, u32[]{:S(2)}) copy-start(bf16[13,2,64,256]{3,2,1,0:T(8,128)(2,1)} %param.30) | copy-start | bytes 2555908
  13.4 0.9 %copy-start.3 = (bf16[64,2048]{1,0:T(8,128)(2,1)S(1)}, bf16[64,2048]{1,0:T(8,128)(2,1)}, u32[]{:S(2)}) copy-start(bf16[64,2048]{1,0:T(8,128)(2,1)} %wattn.1) | copy-start | bytes 786436
  14.4 0.9 %copy-start.4 = (s32[512,1]{1,0:T(8,128)S(1)}, s32[512,1]{1,0:T(8,128)}, u32[]{:S(2)}) copy-start(s32[512,1]{1,0:T(8,128)} %get-tuple-element.15.layout) | copy-start | bytes 6148
  15.3 0.9 copy-start.5
  16.3 0.7 copy-start.18
  16.9 0.6 copy-start.19

commit v2 on v1

v2 whole, which is shorter than its diff:
```python
import jax
import jax.numpy as jnp
from jax import lax
from jax.experimental import pallas as pl
from jax.experimental.pallas import tpu as pltpu
from jax.sharding import PartitionSpec as P

D = 2048
HP = 64
NS = 256
HD = 128
PAGE = 32
SLOTS = 13
ROWS = 32
COLS = 16
MOVES = 4
EPSILON = 1e-05
FLOOR = -1e30
F32 = jnp.float32
BF16 = jnp.bfloat16
I32 = jnp.int32
MESH = pl.DeviceIdType.MESH


def nt(a, b):
    return lax.dot_general(a, b, (((1,), (1,)), ((), ())), preferred_element_type=F32)


def nn(a, b):
    return jnp.dot(a, b, preferred_element_type=F32)


def silu(v):
    return v / (1.0 + jnp.exp(-v))


def mixer_kernel(
    ms, mt, lengths, pt, dtb, alog, dskip,
    ms_v, mt_v, arrival, gain, wdt, cwx, cwbc, conv_x, conv_bc,
    tokens, wz, wx, wbc, wqkv, wssm, wattn, pool, state,
    kv_out, state_out, mixed_out, cx_out, cbc_out,
    send1, recv1, send2, recv2, pcomb, scomb, kvn, stn, convp, cbuf, table_v, table,
    send_r, recv_r, send_b, recv_b, send_s, recv_s, qbuf, fresh, obuf, pbuf, tbuf,
    send_a, recv_a, send_o, recv_o, tokens_v, wz_v, wx_v, shared_v, wssm_v, wattn_v,
    s1_sem, r1_sem, s2_sem, r2_sem, sr_sem, rr_sem, sb_sem, rb_sem, ss_sem, rs_sem,
    sa_sem, ra_sem, so_sem, ro_sem, in_sem, table_sem, out_sem,
):
    row = lax.axis_index("rows")
    col = lax.axis_index("cols")
    core = row & 1
    chip = row >> 1
    plane = row >> 3
    member = row & 7

    barrier = pltpu.get_barrier_semaphore()

    def greet_rows(d, carry):
        pl.semaphore_signal(barrier, inc=1, device_id=((row + d) & (ROWS - 1), col), device_id_type=MESH)
        return carry

    def greet_cols(d, carry):
        pl.semaphore_signal(barrier, inc=1, device_id=(row, (col + d) & (COLS - 1)), device_id_type=MESH)
        return carry

    loads = [
        pltpu.make_async_copy(src, dst, in_sem.at[i])
        for i, (src, dst) in enumerate((
            (tokens, tokens_v), (wz, wz_v), (wx, wx_v),
            (pool, pcomb.at[pl.ds(0, 26)]), (state, scomb.at[pl.ds(0, SLOTS)]),
            (wssm, wssm_v), (wattn, wattn_v),
        ))
    ]
    bc_at = pl.multiple_of(jnp.minimum(col, 3) * 128, 128)
    qkv_at = pl.multiple_of(jnp.maximum(col - 4, 0) * 128, 128)
    load_bc = pltpu.make_async_copy(wbc.at[:, pl.ds(bc_at, 128)], shared_v.at[0], in_sem.at[7])
    load_qkv = pltpu.make_async_copy(wqkv.at[:, pl.ds(qkv_at, 128)], shared_v.at[1], in_sem.at[8])
    for load in loads[:3] + [load_bc, load_qkv] + loads[3:]:
        load.start()
    lax.fori_loop(1, ROWS, greet_rows, 0)
    lax.fori_loop(1, COLS, greet_cols, 0)

    lane = lax.broadcasted_iota(I32, (128, 128), 1)
    sub = lax.broadcasted_iota(I32, (128, 128), 0)
    eye = lane == sub
    line_ms = jnp.concatenate([ms_v[m : m + 1, :] for m in range(MOVES)], axis=1)
    line_mt = jnp.concatenate([mt_v[m : m + 1, :] for m in range(MOVES)], axis=1)
    wide = lambda v: jnp.broadcast_to(v, (128, 128))
    across = lambda v: jnp.sum(v, axis=1, keepdims=True)
    down = lambda v: jnp.sum(v, axis=0, keepdims=True)
    mt_col = across(jnp.where(eye, wide(line_mt), 0))
    ms_col = across(jnp.where(eye, wide(line_ms), 0))
    earlier = (sub & (ROWS - 1)) < (lane & (ROWS - 1))
    rank = down(jnp.where((wide(mt_col) == wide(line_mt)) & earlier, 1, 0))
    place = rank * ROWS + line_mt
    slot_there = down(jnp.where(sub == wide(place), wide(ms_col), 0))
    place_col = across(jnp.where(eye, wide(place), 0))
    kept_at = ((row - sub) & (ROWS - 1)) * 8 + (sub >> 5)
    table_v[...] = jnp.zeros_like(table_v)
    table_v[0:1, :] = down(jnp.where(wide(place_col) == lane, kept_at, 0))
    lane1 = lax.broadcasted_iota(I32, (1, 128), 1)
    owners = jnp.zeros((1, 128), I32)
    for s in range(SLOTS):
        for half in range(2):
            owners = jnp.where(lane1 == pt[half, s], 2 * s + half, owners)
    table_v[1:2, :] = owners
    load_table = pltpu.make_async_copy(table_v, table, table_sem)
    load_table.start()
    source_row = lane1 & (ROWS - 1)
    goes = 16 * line_mt + slot_there
    left = 16 * source_row + line_ms
    request = SLOTS * source_row + line_ms
    q = lax.broadcasted_iota(I32, (512, 128), 0)
    arrived = across(jnp.where(q == goes, request, 0))
    vacated = across(jnp.where(q == left, 1, 0))
    q1 = lax.broadcasted_iota(I32, (512, 1), 0)
    layout = jnp.where(vacated > 0, arrived, (q1 >> 4) * SLOTS + (q1 & 15))
    layout = jnp.where((q1 & 15) < SLOTS, layout, -1)

    onehot = jnp.where(layout == arrival[...], 1.0, 0.0).astype(BF16)
    loads[0].wait()
    picked = nt(onehot, tokens_v[...])
    scaled = (picked * gain[...].astype(F32)).astype(BF16)
    squares = jnp.square(picked)
    squares_hi = squares.astype(BF16)
    squares_lo = (squares - squares_hi.astype(F32)).astype(BF16)
    line64 = lax.broadcasted_iota(I32, (16, 64), 0)
    last = jnp.where(line64 == 15, 1.0, 0.0).astype(BF16)
    steps = wdt[...].astype(F32)
    steps = jnp.where(line64 == 13, steps[0:1], jnp.where(line64 == 14, steps[1:2], 0.0)).astype(BF16)
    extra = nt(steps, scaled) + nt(last, squares_hi) + nt(last, squares_lo)
    for load in (loads[1], loads[2], load_bc, load_qkv):
        load.wait()
    part_z = nn(scaled, wz_v[...]).reshape(4, 8, 16, 128)
    part_x = nn(scaled, wx_v[...]).reshape(4, 8, 16, 128).astype(BF16)
    part_s = nn(scaled, shared_v[jnp.where(col < 4, 0, 1)]).reshape(4, 8, 16, 128).astype(BF16)
    for u in range(4):
        send_r[:, 3 * u] = (part_z[u] + extra[:, 128 * u : 128 * (u + 1)][None]).astype(BF16)
        send_r[:, 3 * u + 1] = part_x[u]
        send_r[:, 3 * u + 2] = part_s[u]

    windows = [conv_x[k].astype(F32) for k in range(3)]
    windows += [conv_bc[k, :, 128 * c : 128 * (c + 1)].astype(F32) for k in range(3) for c in range(4)]
    for i, window in enumerate(windows):
        cbuf[0:SLOTS, i, :] = window
    cbuf[:, 15, :] = jnp.zeros((16, 128), F32)
    convp[...] = cbuf[...].astype(BF16)
    slots = [ms[m, row] for m in range(MOVES)]
    targets = [mt[m, row] for m in range(MOVES)]

    def conv_tile(t, carry):
        at = slots[0]
        for m in range(1, MOVES):
            at = jnp.where(targets[m] == t, slots[m], at)
        send1[t, 4] = convp[at]
        return carry

    lax.fori_loop(0, ROWS, conv_tile, 0)
    loads[3].wait()
    loads[4].wait()

    def cut(m, carry):
        slot = ms[m, row]
        for p in range(16):
            r, l = 16 * (p // 2), 128 * (p % 2)
            send1[2 * p + 1, m] = scomb[slot, r : r + 16, l : l + 128]
        for page in range(2):
            g = pt[page, slot]
            for i in range(8):
                r, l = 16 * (i // 4), 128 * (i % 4)
                send1[2 * (8 * page + i), m] = pcomb[g, r : r + 16, l : l + 128]
        return carry

    lax.fori_loop(0, MOVES, cut, 0)

    pl.semaphore_wait(barrier, ROWS + COLS - 2)

    def reduce_in(d, carry):
        to = (member + d) & 7
        pltpu.make_async_remote_copy(
            send_r.at[to], recv_r.at[d], sr_sem, rr_sem, device_id=(plane * 8 + to, col), device_id_type=MESH
        ).start()
        return carry

    lax.fori_loop(1, 8, reduce_in, 0)

    def hop1(kind):
        def send(d, carry):
            to = 2 * ((chip + d) & 15) + kind

            @pl.when(to != row)
            def _():
                pltpu.make_async_remote_copy(
                    send1.at[to], recv1.at[(to - row) & (ROWS - 1)], s1_sem, r1_sem,
                    device_id=(to, col), device_id_type=MESH,
                ).start()

            return carry

        lax.fori_loop(0, 16, send, 0)

    hop1(0)
    hop1(1)
    recv1[0] = send1[row]
    recv_r[0] = send_r[member]
    load_table.wait()

    away_r = recv_r.at[pl.ds(1, 7)]
    pltpu.make_async_copy(away_r, away_r, rr_sem).wait()
    for u in range(4):
        for j in range(3):
            total = recv_r[0, 3 * u + j].astype(F32)
            for d in range(1, 8):
                total = total + recv_r[d, 3 * u + j].astype(F32)
            send_b[u, j] = total.astype(BF16)

    def reduce_across(d, carry):
        to = (plane + d) & 3
        pltpu.make_async_remote_copy(
            send_b.at[to], recv_b.at[d], sb_sem, rb_sem, device_id=(to * 8 + member, col), device_id_type=MESH
        ).start()
        return carry

    lax.fori_loop(1, 4, reduce_across, 0)
    recv_b[0] = send_b[plane]
    away_b = recv_b.at[pl.ds(1, 3)]
    pltpu.make_async_copy(away_b, away_b, rb_sem).wait()

    zero = jnp.zeros((16, 128), F32)
    sum_z, sum_x, sum_s = (
        recv_b[0, j].astype(F32) + recv_b[1, j].astype(F32) + recv_b[2, j].astype(F32) + recv_b[3, j].astype(F32)
        for j in range(3)
    )
    lane = lax.broadcasted_iota(I32, (16, 128), 1)
    sub = lax.broadcasted_iota(I32, (16, 128), 0)
    low = lane < HP
    mine = lane == sub + 16 * member

    def as_column(k):
        return jnp.sum(jnp.where(mine, jnp.broadcast_to(sum_z[k : k + 1], (16, 128)), 0.0), axis=1, keepdims=True)

    root = jnp.sqrt(as_column(15) / D + EPSILON)
    real = sub < SLOTS
    gate_in = jnp.where(real, sum_z / root, 0.0).astype(BF16).astype(F32)
    value_in = jnp.where(real, sum_x / root, 0.0).astype(BF16)
    step_in = jnp.where(low, as_column(13) / root, as_column(14) / root).astype(BF16).astype(F32)
    send_s[...] = jnp.where(real, sum_s / root, 0.0).astype(BF16)

    def share(d, carry):
        to = (col + d) & (COLS - 1)
        pltpu.make_async_remote_copy(
            send_s, recv_s.at[d], ss_sem, rs_sem, device_id=(row, to), device_id_type=MESH
        ).start()
        return carry

    lax.fori_loop(1, COLS, share, 0)
    recv_s[0] = send_s[...]

    away1 = recv1.at[pl.ds(1, ROWS - 1)]
    pltpu.make_async_copy(away1, away1, r1_sem).wait()

    def pick(t, carry):
        for k in range(MOVES):
            code = table[0, ROWS * k + t]
            send2[t, k] = recv1[(code >> 3) & (ROWS - 1), code & 3]
        return carry

    lax.fori_loop(0, ROWS, pick, 0)

    def hop2(d, carry):
        to = (row + d) & (ROWS - 1)
        pltpu.make_async_remote_copy(
            send2.at[to], recv2.at[d], s2_sem, r2_sem.at[core], device_id=(to, col), device_id_type=MESH
        ).start()
        return carry

    lax.fori_loop(1, ROWS, hop2, 0)
    recv2[0] = send2[row]

    def wait_pieces(kind):
        @pl.when(core == kind)
        def _():
            some = recv2.at[pl.ds(0, 15)]
            pltpu.make_async_copy(some, some, r2_sem.at[kind]).wait()

        @pl.when(core != kind)
        def _():
            some = recv2.at[pl.ds(0, 16)]
            pltpu.make_async_copy(some, some, r2_sem.at[kind]).wait()

    codes = [table[0, ROWS * k + row] for k in range(MOVES)]
    places = []
    for s in range(SLOTS):
        at = jnp.int32(s)
        for k in range(MOVES):
            at = jnp.where(slots[k] == s, SLOTS + k, at)
        places.append(at)
    tiles = [recv1[(code >> 3) & (ROWS - 1), 4].astype(F32) for code in codes]
    window = []
    for i in range(15):
        rows_i = jnp.concatenate([windows[i], jnp.zeros((3, 128), F32)], axis=0)
        for k in range(MOVES):
            rows_i = jnp.where(sub == slots[k], jnp.broadcast_to(tiles[k][i : i + 1], (16, 128)), rows_i)
        window.append(rows_i)

    taps_x = cwx[...].astype(F32)
    taps_bc = cwbc[...].astype(F32)
    conv = value_in.astype(F32) * taps_x[3:4]
    for k in range(3):
        conv = conv + window[k] * taps_x[k : k + 1]
    value_act = silu(conv)
    cx_out[0] = window[1][:SLOTS].astype(BF16)
    cx_out[1] = window[2][:SLOTS].astype(BF16)
    cx_out[2] = value_in[:SLOTS]
    head_lanes = lambda ref: jnp.where(low, ref[0], ref[1])
    raw_step = step_in + head_lanes(dtb)
    step = jnp.maximum(raw_step, 0.0) + jnp.log1p(jnp.exp(-jnp.abs(raw_step)))
    decay = jnp.exp(-jnp.exp(head_lanes(alog)) * step)
    grown = step * value_act

    away_s = recv_s.at[pl.ds(1, COLS - 1)]
    pltpu.make_async_copy(away_s, away_s, rs_sem).wait()

    def chunk(c):
        return recv_s[(col - c) & (COLS - 1)]

    act = []
    for c in range(4):
        new = chunk(c)
        lanes = slice(128 * c, 128 * (c + 1))
        conv = new.astype(F32) * taps_bc[3:4, lanes]
        for k in range(3):
            conv = conv + window[3 + 4 * k + c] * taps_bc[k : k + 1, lanes]
        act.append(silu(conv).astype(BF16))
        cbc_out[0, :, lanes] = window[3 + 4 + c][:SLOTS].astype(BF16)
        cbc_out[1, :, lanes] = window[3 + 8 + c][:SLOTS].astype(BF16)
        cbc_out[2, :, lanes] = new[:SLOTS]
    b_in = jnp.concatenate(act[:2], axis=1)
    c_out = jnp.concatenate(act[2:], axis=1)
    qbuf[...] = jnp.zeros_like(qbuf)
    for h in range(8):
        lanes = slice(128 * (h // 4), 128 * (h // 4 + 1))
        qbuf[:, h, lanes] = chunk(4 + h).astype(F32)
    for j in range(4):
        fresh[:, 0, 128 * j : 128 * (j + 1)] = chunk(12 + j).astype(F32)

    wait_pieces(0)

    def paste_pages(k, carry):
        for p in range(16):
            i = p % 8
            r, l = 16 * (i // 4), 128 * (i % 4)
            pcomb[26 + 2 * k + p // 8, r : r + 16, l : l + 128] = recv2[(row - 2 * p) & (ROWS - 1), k]
        return carry

    lax.fori_loop(0, MOVES, paste_pages, 0)

    def length_of(s):
        request = row * SLOTS + s
        for k in range(MOVES):
            at = (row - (codes[k] >> 3)) & (ROWS - 1)
            request = jnp.where(slots[k] == s, at * SLOTS + ms[codes[k] & 3, at], request)
        return lengths[request]

    line = lax.broadcasted_iota(I32, (PAGE, 512), 0)

    def page(g, carry):
        entry = table[1, g]
        s, half = entry >> 1, entry & 1
        at = g
        for k in range(MOVES):
            at = jnp.where(slots[k] == s, 26 + 2 * k + half, at)
        length = length_of(s)
        logical = length >> 5
        here = ((logical & (COLS - 1)) == col) & ((logical >> 4) == half)
        offset = jnp.where(here, length & (PAGE - 1), -1)
        kvn[g] = jnp.where(line == offset, fresh[s].astype(F32), pcomb[at].astype(F32)).astype(BF16)
        return carry

    lax.fori_loop(0, 26, page, 0)
    kv_copy = pltpu.make_async_copy(kvn, kv_out, out_sem.at[0])
    kv_copy.start()

    for ref in (obuf, pbuf, tbuf):
        ref[...] = jnp.zeros_like(ref)
    token = lax.broadcasted_iota(I32, (8, 64), 1)
    position = (token >> 5) * (COLS * PAGE) + col * PAGE + (token & (PAGE - 1))
    head = lax.broadcasted_iota(I32, (8, 128), 0)
    for s in range(SLOTS):
        both = jnp.concatenate([kvn[pt[0, s]], kvn[pt[1, s]]], axis=0)
        scores = nt(qbuf[s].astype(BF16), both[:, :256]) * (HD**-0.5)
        live = position <= length_of(s)
        peak = jnp.max(jnp.where(live, scores, FLOOR), axis=1, keepdims=True)
        weights = jnp.where(live, jnp.exp(scores - peak), 0.0)
        summed = nn(weights.astype(BF16), both[:, 256:])
        obuf[:, s, :] = jnp.where(head < 4, summed[:, :128], summed[:, 128:])
        pbuf[:, s, :] = jnp.broadcast_to(peak, (8, 128))
        tbuf[:, s, :] = jnp.broadcast_to(jnp.sum(weights, axis=1, keepdims=True), (8, 128))
    for h in range(8):
        stats = jnp.where(lane == HP, pbuf[h], tbuf[h])
        send_a[2 * h] = jnp.where(low, obuf[h], stats)
        send_a[2 * h + 1] = jnp.where(low, pltpu.roll(obuf[h], HP, 1), stats)

    def attend(d, carry):
        to = (col + d) & (COLS - 1)
        pltpu.make_async_remote_copy(
            send_a.at[to], recv_a.at[d], sa_sem, ra_sem, device_id=(row, to), device_id_type=MESH
        ).start()
        return carry

    lax.fori_loop(1, COLS, attend, 0)
    recv_a[0] = send_a[col]

    wait_pieces(1)

    def paste_states(k, carry):
        for p in range(16):
            r, l = 16 * (p // 2), 128 * (p % 2)
            scomb[SLOTS + k, r : r + 16, l : l + 128] = recv2[(row - 2 * p - 1) & (ROWS - 1), k]
        return carry

    lax.fori_loop(0, MOVES, paste_states, 0)
    read = zero
    for s in range(SLOTS):
        read = jnp.where(sub == s, nt(c_out, scomb[places[s]]), read)
    b_dot_c = jnp.sum(b_in.astype(F32) * c_out.astype(F32), axis=1, keepdims=True)
    readout = decay * read + grown * b_dot_c + head_lanes(dskip) * value_act
    gated = (readout * silu(gate_in)).astype(BF16)
    loads[5].wait()
    loads[6].wait()
    out_terms = nn(gated, wssm_v[...])

    away_a = recv_a.at[pl.ds(1, COLS - 1)]
    pltpu.make_async_copy(away_a, away_a, ra_sem).wait()
    top = recv_a[0]
    for d in range(1, COLS):
        top = jnp.maximum(top, recv_a[d])
    top = top[:, HP : HP + 1]
    gathered = zero
    for d in range(COLS):
        part = recv_a[d]
        gathered = gathered + part * jnp.exp(part[:, HP : HP + 1] - top)
    attended = (gathered / gathered[:, HP + 1 : HP + 2]).astype(BF16)
    out_terms = out_terms + nn(attended[:, :HP], wattn_v[...])
    for c in range(COLS):
        send_o[c] = out_terms[:, 128 * c : 128 * (c + 1)].astype(BF16)

    def project(d, carry):
        to = (col + d) & (COLS - 1)
        pltpu.make_async_remote_copy(
            send_o.at[to], recv_o.at[d], so_sem, ro_sem, device_id=(row, to), device_id_type=MESH
        ).start()
        return carry

    lax.fori_loop(1, COLS, project, 0)
    recv_o[0] = send_o[col]

    columns = jnp.concatenate([grown, decay, jnp.zeros((96, 128), F32)], axis=0).T
    for s in range(SLOTS):
        old = scomb[places[s]].astype(F32)
        new = columns[:, 16 + s : 17 + s] * old + columns[:, s : s + 1] * b_in[s : s + 1].astype(F32)
        stn[s] = new.astype(BF16)
    state_copy_out = pltpu.make_async_copy(stn, state_out, out_sem.at[1])
    state_copy_out.start()

    away_o = recv_o.at[pl.ds(1, COLS - 1)]
    pltpu.make_async_copy(away_o, away_o, ro_sem).wait()
    mixed = zero
    for d in range(COLS):
        mixed = mixed + recv_o[d].astype(F32)
    mixed_out[...] = mixed[:SLOTS].astype(BF16)

    sent1 = send1.at[pl.ds(0, ROWS - 1)]
    pltpu.make_async_copy(sent1, sent1, s1_sem).wait()
    sent2 = send2.at[pl.ds(0, ROWS - 1)]
    pltpu.make_async_copy(sent2, sent2, s2_sem).wait()
    sent_r = send_r.at[pl.ds(0, 7)]
    pltpu.make_async_copy(sent_r, sent_r, sr_sem).wait()
    sent_b = send_b.at[pl.ds(0, 3)]
    pltpu.make_async_copy(sent_b, sent_b, sb_sem).wait()
    for sem, ref in ((ss_sem, recv_s), (sa_sem, send_a), (so_sem, send_o)):
        sent = ref.at[pl.ds(0, COLS - 1)]
        pltpu.make_async_copy(sent, sent, sem).wait()
    kv_copy.wait()
    state_copy_out.wait()


def emit_kernel(*refs):
    made, out, held, sem = refs[:5], refs[5:10], refs[10:15], refs[15]
    reads = [pltpu.make_async_copy(made[i], held[i], sem.at[i]) for i in range(5)]
    writes = [pltpu.make_async_copy(held[i], out[i], sem.at[5 + i]) for i in range(5)]
    for read in reads:
        read.start()
    for i in (2, 3, 4, 0, 1):
        reads[i].wait()
        writes[i].start()
    for write in writes:
        write.wait()


def local(
    tokens, arrival, cache_lengths, move_slot, move_target, page_table, kv_pool, ssm_state, conv_x, conv_bc,
    norm_gain, weight_z, weight_x, weight_dt, weight_bc, weight_qkv, conv_weight_x, conv_weight_bc,
    dt_bias, a_log, d_skip, weight_ssm_out, weight_attn_out,
):
    vmem = pl.BlockSpec(memory_space=pltpu.VMEM)
    smem = pl.BlockSpec(memory_space=pltpu.SMEM)
    anywhere = pl.BlockSpec(memory_space=pl.ANY)
    ms, mt = move_slot.T, move_target.T
    pt = page_table.reshape(SLOTS, 2).T
    dma = pltpu.SemaphoreType.DMA
    results = (
        jax.ShapeDtypeStruct((26, PAGE, 512), BF16),
        jax.ShapeDtypeStruct((SLOTS, 128, NS), BF16),
        jax.ShapeDtypeStruct((SLOTS, 128), BF16),
        jax.ShapeDtypeStruct((3, SLOTS, 128), BF16),
        jax.ShapeDtypeStruct((3, SLOTS, 512), BF16),
    )
    tile = lambda *lead: pltpu.VMEM((*lead, 16, 128), BF16)
    made = pl.pallas_call(
        mixer_kernel,
        out_shape=results,
        in_specs=[smem] * 7 + [vmem] * 9 + [anywhere] * 9,
        out_specs=(anywhere, anywhere, vmem, vmem, vmem),
        scratch_shapes=[
            tile(ROWS, 5),
            tile(ROWS, 5),
            tile(ROWS, MOVES),
            tile(ROWS, MOVES),
            pltpu.VMEM((34, PAGE, 512), BF16),
            pltpu.VMEM((SLOTS + MOVES, 128, NS), BF16),
            pltpu.VMEM((26, PAGE, 512), BF16),
            pltpu.VMEM((SLOTS, 128, NS), BF16),
            tile(16),
            pltpu.VMEM((16, 16, 128), F32),
            pltpu.VMEM((8, 128), I32),
            pltpu.SMEM((8, 128), I32),
            tile(8, 12),
            tile(8, 12),
            tile(4, 3),
            tile(4, 3),
            tile(),
            tile(COLS),
            pltpu.VMEM((16, 8, 256), F32),
            pltpu.VMEM((16, 1, 512), F32),
            pltpu.VMEM((8, 16, 128), F32),
            pltpu.VMEM((8, 16, 128), F32),
            pltpu.VMEM((8, 16, 128), F32),
            pltpu.VMEM((COLS, 16, 128), F32),
            pltpu.VMEM((COLS, 16, 128), F32),
            tile(COLS),
            tile(COLS),
            pltpu.VMEM((64, 416), BF16),
            pltpu.VMEM((64, 128), BF16),
            pltpu.VMEM((64, 128), BF16),
            pltpu.VMEM((2, 64, 128), BF16),
            pltpu.VMEM((128, D), BF16),
            pltpu.VMEM((64, D), BF16),
        ]
        + [dma] * 3
        + [dma((2,))]
        + [dma] * 10
        + [dma((9,)), dma, dma((2,))],
        compiler_params=pltpu.CompilerParams(
            collective_id=0, has_side_effects=True, vmem_limit_bytes=60 * 1024 * 1024
        ),
        name="mixer",
    )(
        ms, mt, cache_lengths, pt, dt_bias, a_log, d_skip,
        ms, mt, arrival.reshape(1, 416), norm_gain.reshape(1, 64), weight_dt.T, conv_weight_x, conv_weight_bc,
        conv_x.transpose(1, 0, 2), conv_bc.transpose(1, 0, 2),
        tokens.T, weight_z, weight_x, weight_bc, weight_qkv, weight_ssm_out, weight_attn_out,
        kv_pool.reshape(26, PAGE, 512), ssm_state.reshape(SLOTS, 128, NS),
    )
    kv_next, state_next, mixed, cx, cbc = pl.pallas_call(
        emit_kernel,
        out_shape=results,
        in_specs=[anywhere] * 5,
        out_specs=(anywhere,) * 5,
        scratch_shapes=[pltpu.VMEM(r.shape, r.dtype) for r in results] + [dma((10,))],
        name="emit",
    )(*made)
    return (
        mixed,
        state_next.reshape(SLOTS, 2, HP, NS),
        cx.transpose(1, 0, 2),
        cbc.transpose(1, 0, 2),
        kv_next.reshape(26, 1, PAGE, 512),
    )


def solution(mesh):
    in_specs = (
        P(None, "rows"), P(), P(), P(), P(), P("rows", "cols", None, None), P("rows", "cols", None, None),
        P("rows", "cols", None, None), P("rows", None, "cols"), P("rows", None, None), P("rows"),
        P("rows", "cols"), P("rows", "cols"), P("rows", "cols"), P("rows", None), P("rows", None),
        P(None, "cols"), P(), P("cols"), P("cols"), P("cols"), P("cols", None), P("cols", None),
    )
    out_specs = (
        P("rows", "cols"),
        P("rows", "cols", None, None),
        P("rows", None, "cols"),
        P("rows", None, None),
        P("rows", "cols", None, None),
    )
    return jax.shard_map(local, mesh=mesh, in_specs=in_specs, out_specs=out_specs, check_vma=False)
```

time: 94.5 us -> 68.4 us (0.72)
  local copies, waits for them, and re-layouts: 18.4 us -> 0 us
  Pallas kernels: 74.6 us -> 67.5 us
    unnamed x51 -> x0, local copies, waits for them, and re-layouts: 15.5 us -> none
    pallas_call x2, Pallas kernels: 74.6 us -> 67.5 us  [the longest x1 64.9 us: local(): pl.pallas_call(mixer_kernel, out_shape=results, in_specs=[smem] * 7 + [vm...]
    another operation x2 -> x0, local copies, waits for them, and re-layouts: 1.24 us -> none  [the longest x1 0.62 us: local(): ms.reshape(1, 128)]
where the time goes in v2:
time: 68.4 us; the launch traced here: 68.1 us
  Pallas kernels  67.5 us (99%)
    pallas_call x1, Pallas kernels, local(): pl.pallas_call(mixer_kernel, out_shape=results, in_specs=[smem] * 7 + [vm...  64.9 us
    pallas_call x1, Pallas kernels, local(): pl.pallas_call(emit_kernel, out_shape=results, in_specs=[anywhere] * 5, o...  2.62 us

profile of v2, /device:TPU:6, one launch (start us, length us, event | category | flops | bytes accessed | tf_op | source)
XLA Modules:
  0.0 68.1 jit_solution(4331317341698260183)
XLA Ops:
  0.6 64.9 %mixer.1 = (bf16[26,32,512]{2,1,0:T(8,128)(2,1)}, bf16[13,128,256]{2,1,0:T(8,128)(2,1)}, bf16[13,128]{1,0:T(8,128)(2,1)}, bf16[3,13,128]{2,1,0:T(8,128)(2,1)}, bf16[3,13,512]{2,1,0:T(8,128)(2,1)}) custom-call(s32[4,32]{1,0:T(4,128)} %bitcast.24, s32[4,32]{1,0:T(4,128)} %bitcast.26, s32[416]{0:T(512)} %lengths.1, s32[2,13]{1,0:T(2,128)} %bitcast.29, f32[2]{0:T(128)} %dtb.1, ...), custom_call_target="tpu_custom_call" | custom-call | tf_op jit(solution)/shard_map/mixer/pallas_call | solution.py:519
  65.5 2.6 %emit.1 = (bf16[26,32,512]{2,1,0:T(8,128)(2,1)}, bf16[13,128,256]{2,1,0:T(8,128)(2,1)}, bf16[13,128]{1,0:T(8,128)(2,1)}, bf16[3,13,128]{2,1,0:T(8,128)(2,1)}, bf16[3,13,512]{2,1,0:T(8,128)(2,1)}) custom-call(bf16[26,32,512]{2,1,0:T(8,128)(2,1)} %get-tuple-element.15.refs_0_, bf16[13,128,256]{2,1,0:T(8,128)(2,1)} %get-tuple-element.16.refs_1_, ...), custom_call_target="tpu_custom_call" | custom-call | tf_op jit(solution)/shard_map/emit/pallas_call | solution.py:574

commit v3 on v2

--- a/solution.py
+++ b/solution.py
@@ -39,8 +39,8 @@
     ms_v, mt_v, arrival, gain, wdt, cwx, cwbc, conv_x, conv_bc,
     tokens, wz, wx, wbc, wqkv, wssm, wattn, pool, state,
     kv_out, state_out, mixed_out, cx_out, cbc_out,
-    send1, recv1, send2, recv2, pcomb, scomb, kvn, stn, convp, cbuf, table_v, table,
-    send_r, recv_r, send_b, recv_b, send_s, recv_s, qbuf, fresh, obuf, pbuf, tbuf,
+    send1, recv1, send2, recv2, pcomb, scomb, kvn, stn, leave, going, passing, came, table_v, table,
+    send_r, recv_r, send_b, recv_b, send_s, recv_s, qbuf, fresh,
     send_a, recv_a, send_o, recv_o, tokens_v, wz_v, wx_v, shared_v, wssm_v, wattn_v,
     s1_sem, r1_sem, s2_sem, r2_sem, sr_sem, rr_sem, sb_sem, rb_sem, ss_sem, rs_sem,
     sa_sem, ra_sem, so_sem, ro_sem, in_sem, table_sem, out_sem,
@@ -74,10 +74,58 @@
     qkv_at = pl.multiple_of(jnp.maximum(col - 4, 0) * 128, 128)
     load_bc = pltpu.make_async_copy(wbc.at[:, pl.ds(bc_at, 128)], shared_v.at[0], in_sem.at[7])
     load_qkv = pltpu.make_async_copy(wqkv.at[:, pl.ds(qkv_at, 128)], shared_v.at[1], in_sem.at[8])
-    for load in loads[:3] + [load_bc, load_qkv] + loads[3:]:
+    for load in loads[3:5] + loads[:3] + [load_bc, load_qkv] + loads[5:]:
         load.start()
     lax.fori_loop(1, ROWS, greet_rows, 0)
     lax.fori_loop(1, COLS, greet_cols, 0)
+
+    slots = [ms[m, row] for m in range(MOVES)]
+    targets = [mt[m, row] for m in range(MOVES)]
+
+    def cut_pages(m, carry):
+        slot = ms[m, row]
+        for page in range(2):
+            g = pt[page, slot]
+            for i in range(8):
+                r, l = 16 * (i // 4), 128 * (i % 4)
+                send1[2 * (8 * page + i), m] = pcomb[g, r : r + 16, l : l + 128]
+        return carry
+
+    loads[3].wait()
+    lax.fori_loop(0, MOVES, cut_pages, 0)
+
+    pl.semaphore_wait(barrier, ROWS + COLS - 2)
+
+    def hop1(kind):
+        def send(d, carry):
+            to = 2 * ((chip + d) & 15) + kind
+
+            @pl.when(to != row)
+            def _():
+                pltpu.make_async_remote_copy(
+                    send1.at[to], recv1.at[(to - row) & (ROWS - 1)], s1_sem, r1_sem,
+                    device_id=(to, col), device_id_type=MESH,
+                ).start()
+
+            return carry
+
+        lax.fori_loop(0, 16, send, 0)
+
+    hop1(0)
+
+    def cut_states(m, carry):
+        slot = ms[m, row]
+        for p in range(16):
+            r, l = 16 * (p // 2), 128 * (p % 2)
+            send1[2 * p + 1, m] = scomb[slot, r : r + 16, l : l + 128]
+        return carry
+
+    loads[4].wait()
+    lax.fori_loop(0, MOVES, cut_states, 0)
+
+    @pl.when(core == 1)
+    def _():
+        hop1(1)
 
     lane = lax.broadcasted_iota(I32, (128, 128), 1)
     sub = lax.broadcasted_iota(I32, (128, 128), 0)
@@ -133,46 +181,33 @@
     part_z = nn(scaled, wz_v[...]).reshape(4, 8, 16, 128)
     part_x = nn(scaled, wx_v[...]).reshape(4, 8, 16, 128).astype(BF16)
     part_s = nn(scaled, shared_v[jnp.where(col < 4, 0, 1)]).reshape(4, 8, 16, 128).astype(BF16)
+    windows = [conv_x[k].astype(F32) for k in range(3)]
+    windows += [conv_bc[k, :, 128 * c : 128 * (c + 1)].astype(F32) for k in range(3) for c in range(4)]
+    lane16 = lax.broadcasted_iota(I32, (16, 128), 1)
+    quarter = lane16 >> 5
+    pad = jnp.zeros((3, 128), F32)
+    bc_lanes = pl.ds(pl.multiple_of((col >> 2) * 128, 128), 128)
+    taps = jnp.zeros((16, 128), F32)
+    for k in range(3):
+        tap = jnp.concatenate([conv_bc[k, :, bc_lanes].astype(F32), pad], axis=0)
+        taps = jnp.where(quarter == k, pltpu.roll(tap, (32 * (k - (col & 3))) & 127, 1), taps)
+        leave[:, k, :] = jnp.concatenate([windows[k], pad], axis=0)
+    leave[:, 3, :] = taps
+
+    def conv_rows(m, carry):
+        for u in range(4):
+            at = slots[0]
+            for k in range(1, MOVES):
+                at = jnp.where(targets[k] == 8 * u + m, slots[k], at)
+            going[m, 4 * u : 4 * u + 4, :] = leave[at][0:4]
+        return carry
+
+    lax.fori_loop(0, 8, conv_rows, 0)
+    send_r[:, 12] = going[...].astype(BF16)
     for u in range(4):
         send_r[:, 3 * u] = (part_z[u] + extra[:, 128 * u : 128 * (u + 1)][None]).astype(BF16)
         send_r[:, 3 * u + 1] = part_x[u]
         send_r[:, 3 * u + 2] = part_s[u]
-
-    windows = [conv_x[k].astype(F32) for k in range(3)]
-    windows += [conv_bc[k, :, 128 * c : 128 * (c + 1)].astype(F32) for k in range(3) for c in range(4)]
-    for i, window in enumerate(windows):
-        cbuf[0:SLOTS, i, :] = window
-    cbuf[:, 15, :] = jnp.zeros((16, 128), F32)
-    convp[...] = cbuf[...].astype(BF16)
-    slots = [ms[m, row] for m in range(MOVES)]
-    targets = [mt[m, row] for m in range(MOVES)]
-
-    def conv_tile(t, carry):
-        at = slots[0]
-        for m in range(1, MOVES):
-            at = jnp.where(targets[m] == t, slots[m], at)
-        send1[t, 4] = convp[at]
-        return carry
-
-    lax.fori_loop(0, ROWS, conv_tile, 0)
-    loads[3].wait()
-    loads[4].wait()
-
-    def cut(m, carry):
-        slot = ms[m, row]
-        for p in range(16):
-            r, l = 16 * (p // 2), 128 * (p % 2)
-            send1[2 * p + 1, m] = scomb[slot, r : r + 16, l : l + 128]
-        for page in range(2):
-            g = pt[page, slot]
-            for i in range(8):
-                r, l = 16 * (i // 4), 128 * (i % 4)
-                send1[2 * (8 * page + i), m] = pcomb[g, r : r + 16, l : l + 128]
-        return carry
-
-    lax.fori_loop(0, MOVES, cut, 0)
-
-    pl.semaphore_wait(barrier, ROWS + COLS - 2)
 
     def reduce_in(d, carry):
         to = (member + d) & 7
@@ -183,25 +218,8 @@
 
     lax.fori_loop(1, 8, reduce_in, 0)
 
-    def hop1(kind):
-        def send(d, carry):
-            to = 2 * ((chip + d) & 15) + kind
-
-            @pl.when(to != row)
-            def _():
-                pltpu.make_async_remote_copy(
-                    send1.at[to], recv1.at[(to - row) & (ROWS - 1)], s1_sem, r1_sem,
-                    device_id=(to, col), device_id_type=MESH,
-                ).start()
-
-            return carry
-
-        lax.fori_loop(0, 16, send, 0)
-
-    hop1(0)
-    hop1(1)
-    recv1[0] = send1[row]
     recv_r[0] = send_r[member]
+
     load_table.wait()
 
     away_r = recv_r.at[pl.ds(1, 7)]
@@ -212,6 +230,13 @@
             for d in range(1, 8):
                 total = total + recv_r[d, 3 * u + j].astype(F32)
             send_b[u, j] = total.astype(BF16)
+    for d in range(8):
+        rows_d = recv_r[d, 12].astype(F32)
+        for u in range(4):
+            passing[u, 4 * d : 4 * d + 4, :] = rows_d[4 * u : 4 * u + 4]
+    for u in range(4):
+        send_b[u, 3] = passing[u, 0:16].astype(BF16)
+        send_b[u, 4] = passing[u, 16:32].astype(BF16)
 
     def reduce_across(d, carry):
         to = (plane + d) & 3
@@ -221,6 +246,37 @@
         return carry
 
     lax.fori_loop(1, 4, reduce_across, 0)
+
+    away1 = recv1.at[pl.ds(1, ROWS - 1)]
+
+    def pick(t, carry):
+        for k in range(MOVES):
+            code = table[0, ROWS * k + t]
+            send2[t, k] = recv1[(code >> 3) & (ROWS - 1), code & 3]
+        return carry
+
+    def hop2(d, carry):
+        to = (row + d) & (ROWS - 1)
+        pltpu.make_async_remote_copy(
+            send2.at[to], recv2.at[d], s2_sem, r2_sem.at[core], device_id=(to, col), device_id_type=MESH
+        ).start()
+        return carry
+
+    def second_hop(kind):
+        @pl.when(core == kind)
+        def _():
+            recv1[0] = send1[row]
+            pltpu.make_async_copy(away1, away1, r1_sem).wait()
+            lax.fori_loop(0, ROWS, pick, 0)
+            lax.fori_loop(1, ROWS, hop2, 0)
+            recv2[0] = send2[row]
+
+    second_hop(0)
+
+    @pl.when(core == 0)
+    def _():
+        hop1(1)
+
     recv_b[0] = send_b[plane]
     away_b = recv_b.at[pl.ds(1, 3)]
     pltpu.make_async_copy(away_b, away_b, rb_sem).wait()
@@ -243,7 +299,25 @@
     gate_in = jnp.where(real, sum_z / root, 0.0).astype(BF16).astype(F32)
     value_in = jnp.where(real, sum_x / root, 0.0).astype(BF16)
     step_in = jnp.where(low, as_column(13) / root, as_column(14) / root).astype(BF16).astype(F32)
-    send_s[...] = jnp.where(real, sum_s / root, 0.0).astype(BF16)
+
+    for e in range(4):
+        for half in range(2):
+            rows_e = recv_b[e, 3 + half].astype(F32)
+            for d in range(4):
+                came[8 * e + 4 * half + d, 0:4, :] = rows_e[4 * d : 4 * d + 4]
+    codes = [table[0, ROWS * k + row] for k in range(MOVES)]
+    tiles = []
+    for code in codes:
+        at = (row - (code >> 3)) & (ROWS - 1)
+        tiles.append(came[8 * ((plane - (at >> 3)) & 3) + ((member - (at & 7)) & 7)])
+    quarter = lane >> 5
+    bc_rows = zero
+    for k in range(3):
+        for m in range(MOVES):
+            moved = jnp.broadcast_to(tiles[m][3:4], (16, 128))
+            moved = moved if m == k else pltpu.roll(moved, (32 * (m - k)) % 128, 1)
+            bc_rows = jnp.where((sub == SLOTS + k) & (quarter == m), moved, bc_rows)
+    send_s[...] = jnp.where(real, sum_s / root, bc_rows).astype(BF16)
 
     def share(d, carry):
         to = (col + d) & (COLS - 1)
@@ -255,26 +329,7 @@
     lax.fori_loop(1, COLS, share, 0)
     recv_s[0] = send_s[...]
 
-    away1 = recv1.at[pl.ds(1, ROWS - 1)]
-    pltpu.make_async_copy(away1, away1, r1_sem).wait()
-
-    def pick(t, carry):
-        for k in range(MOVES):
-            code = table[0, ROWS * k + t]
-            send2[t, k] = recv1[(code >> 3) & (ROWS - 1), code & 3]
-        return carry
-
-    lax.fori_loop(0, ROWS, pick, 0)
-
-    def hop2(d, carry):
-        to = (row + d) & (ROWS - 1)
-        pltpu.make_async_remote_copy(
-            send2.at[to], recv2.at[d], s2_sem, r2_sem.at[core], device_id=(to, col), device_id_type=MESH
-        ).start()
-        return carry
-
-    lax.fori_loop(1, ROWS, hop2, 0)
-    recv2[0] = send2[row]
+    second_hop(1)
 
     def wait_pieces(kind):
         @pl.when(core == kind)
@@ -287,20 +342,13 @@
             some = recv2.at[pl.ds(0, 16)]
             pltpu.make_async_copy(some, some, r2_sem.at[kind]).wait()
 
-    codes = [table[0, ROWS * k + row] for k in range(MOVES)]
-    places = []
-    for s in range(SLOTS):
-        at = jnp.int32(s)
-        for k in range(MOVES):
-            at = jnp.where(slots[k] == s, SLOTS + k, at)
-        places.append(at)
-    tiles = [recv1[(code >> 3) & (ROWS - 1), 4].astype(F32) for code in codes]
-    window = []
-    for i in range(15):
+    def with_arrived(i, rows_of):
         rows_i = jnp.concatenate([windows[i], jnp.zeros((3, 128), F32)], axis=0)
         for k in range(MOVES):
-            rows_i = jnp.where(sub == slots[k], jnp.broadcast_to(tiles[k][i : i + 1], (16, 128)), rows_i)
-        window.append(rows_i)
+            rows_i = jnp.where(sub == slots[k], jnp.broadcast_to(rows_of(k), (16, 128)), rows_i)
+        return rows_i
+
+    window = [with_arrived(i, lambda k, i=i: tiles[k][i : i + 1]) for i in range(3)]
 
     taps_x = cwx[...].astype(F32)
     taps_bc = cwbc[...].astype(F32)
@@ -323,19 +371,32 @@
     def chunk(c):
         return recv_s[(col - c) & (COLS - 1)]
 
+    for c in range(4):
+        joined = []
+        for m in range(MOVES):
+            rows_m = zero
+            for j in range(4):
+                other = chunk(4 * c + j).astype(F32)
+                other = other if j == m else pltpu.roll(other, (32 * (j - m)) % 128, 1)
+                rows_m = jnp.where(quarter == j, other, rows_m)
+            joined.append(rows_m)
+        window += [
+            with_arrived(3 + 4 * k + c, lambda m, k=k: joined[m][SLOTS + k : SLOTS + k + 1]) for k in range(3)
+        ]
     act = []
     for c in range(4):
         new = chunk(c)
         lanes = slice(128 * c, 128 * (c + 1))
         conv = new.astype(F32) * taps_bc[3:4, lanes]
         for k in range(3):
-            conv = conv + window[3 + 4 * k + c] * taps_bc[k : k + 1, lanes]
+            conv = conv + window[3 + 3 * c + k] * taps_bc[k : k + 1, lanes]
         act.append(silu(conv).astype(BF16))
-        cbc_out[0, :, lanes] = window[3 + 4 + c][:SLOTS].astype(BF16)
-        cbc_out[1, :, lanes] = window[3 + 8 + c][:SLOTS].astype(BF16)
+        cbc_out[0, :, lanes] = window[3 + 3 * c + 1][:SLOTS].astype(BF16)
+        cbc_out[1, :, lanes] = window[3 + 3 * c + 2][:SLOTS].astype(BF16)
         cbc_out[2, :, lanes] = new[:SLOTS]
     b_in = jnp.concatenate(act[:2], axis=1)
     c_out = jnp.concatenate(act[2:], axis=1)
+
     qbuf[...] = jnp.zeros_like(qbuf)
     for h in range(8):
         lanes = slice(128 * (h // 4), 128 * (h // 4 + 1))
@@ -343,17 +404,6 @@
     for j in range(4):
         fresh[:, 0, 128 * j : 128 * (j + 1)] = chunk(12 + j).astype(F32)
 
-    wait_pieces(0)
-
-    def paste_pages(k, carry):
-        for p in range(16):
-            i = p % 8
-            r, l = 16 * (i // 4), 128 * (i % 4)
-            pcomb[26 + 2 * k + p // 8, r : r + 16, l : l + 128] = recv2[(row - 2 * p) & (ROWS - 1), k]
-        return carry
-
-    lax.fori_loop(0, MOVES, paste_pages, 0)
-
     def length_of(s):
         request = row * SLOTS + s
         for k in range(MOVES):
@@ -363,52 +413,90 @@
 
     line = lax.broadcasted_iota(I32, (PAGE, 512), 0)
 
-    def page(g, carry):
-        entry = table[1, g]
-        s, half = entry >> 1, entry & 1
-        at = g
-        for k in range(MOVES):
-            at = jnp.where(slots[k] == s, 26 + 2 * k + half, at)
+    def page(at, s, half):
         length = length_of(s)
         logical = length >> 5
         here = ((logical & (COLS - 1)) == col) & ((logical >> 4) == half)
         offset = jnp.where(here, length & (PAGE - 1), -1)
-        kvn[g] = jnp.where(line == offset, fresh[s].astype(F32), pcomb[at].astype(F32)).astype(BF16)
-        return carry
-
-    lax.fori_loop(0, 26, page, 0)
-    kv_copy = pltpu.make_async_copy(kvn, kv_out, out_sem.at[0])
+        return jnp.where(line == offset, fresh[s].astype(F32), pcomb[at].astype(F32)).astype(BF16)
+
+    def own_page(g, carry):
+        entry = table[1, g]
+        kvn[g] = page(g, entry >> 1, entry & 1)
+        return carry
+
+    lax.fori_loop(0, 26, own_page, 0)
+    kv_copy = pltpu.make_async_copy(kvn.at[pl.ds(0, 26)], kv_out.at[pl.ds(0, 26)], out_sem.at[0])
     kv_copy.start()
 
-    for ref in (obuf, pbuf, tbuf):
-        ref[...] = jnp.zeros_like(ref)
     token = lax.broadcasted_iota(I32, (8, 64), 1)
     position = (token >> 5) * (COLS * PAGE) + col * PAGE + (token & (PAGE - 1))
     head = lax.broadcasted_iota(I32, (8, 128), 0)
-    for s in range(SLOTS):
-        both = jnp.concatenate([kvn[pt[0, s]], kvn[pt[1, s]]], axis=0)
+    lane8 = lax.broadcasted_iota(I32, (8, 128), 1)
+
+    def attention(s, first, second):
+        both = jnp.concatenate([first, second], axis=0)
         scores = nt(qbuf[s].astype(BF16), both[:, :256]) * (HD**-0.5)
         live = position <= length_of(s)
         peak = jnp.max(jnp.where(live, scores, FLOOR), axis=1, keepdims=True)
         weights = jnp.where(live, jnp.exp(scores - peak), 0.0)
         summed = nn(weights.astype(BF16), both[:, 256:])
-        obuf[:, s, :] = jnp.where(head < 4, summed[:, :128], summed[:, 128:])
-        pbuf[:, s, :] = jnp.broadcast_to(peak, (8, 128))
-        tbuf[:, s, :] = jnp.broadcast_to(jnp.sum(weights, axis=1, keepdims=True), (8, 128))
+        summed = jnp.where(head < 4, summed[:, :128], summed[:, 128:])
+        stats = jnp.where(lane8 == HP, peak, jnp.sum(weights, axis=1, keepdims=True))
+        return jnp.where(lane8 < HP, summed, stats), jnp.where(lane8 < HP, pltpu.roll(summed, HP, 1), stats)
+
+    for s in range(SLOTS):
+        send_a[:, 0, s, :], send_a[:, 1, s, :] = attention(s, kvn[pt[0, s]], kvn[pt[1, s]])
+    for s in range(SLOTS, 16):
+        send_a[:, 0, s, :] = jnp.zeros((8, 128), F32)
+        send_a[:, 1, s, :] = jnp.zeros((8, 128), F32)
+
+    wait_pieces(0)
+
+    def paste_pages(k, carry):
+        for p in range(16):
+            i = p % 8
+            r, l = 16 * (i // 4), 128 * (i % 4)
+            pcomb[26 + 2 * k + p // 8, r : r + 16, l : l + 128] = recv2[(row - 2 * p) & (ROWS - 1), k]
+        for half in range(2):
+            kvn[26 + 2 * k + half] = page(26 + 2 * k + half, ms[k, row], half)
+        return carry
+
+    lax.fori_loop(0, MOVES, paste_pages, 0)
+    kv_copy2 = pltpu.make_async_copy(kvn.at[pl.ds(26, 8)], kv_out.at[pl.ds(26, 8)], out_sem.at[1])
+    kv_copy2.start()
+    found = [attention(slots[k], kvn[26 + 2 * k], kvn[27 + 2 * k]) for k in range(MOVES)]
     for h in range(8):
-        stats = jnp.where(lane == HP, pbuf[h], tbuf[h])
-        send_a[2 * h] = jnp.where(low, obuf[h], stats)
-        send_a[2 * h + 1] = jnp.where(low, pltpu.roll(obuf[h], HP, 1), stats)
+        for half in range(2):
+            tile = send_a[h, half]
+            for k in range(MOVES):
+                tile = jnp.where(sub == slots[k], jnp.broadcast_to(found[k][half][h : h + 1], (16, 128)), tile)
+            send_a[h, half] = tile
 
     def attend(d, carry):
         to = (col + d) & (COLS - 1)
         pltpu.make_async_remote_copy(
-            send_a.at[to], recv_a.at[d], sa_sem, ra_sem, device_id=(row, to), device_id_type=MESH
+            send_a.at[to >> 1, to & 1], recv_a.at[d], sa_sem, ra_sem, device_id=(row, to), device_id_type=MESH
         ).start()
         return carry
 
     lax.fori_loop(1, COLS, attend, 0)
-    recv_a[0] = send_a[col]
+    recv_a[0] = send_a[col >> 1, col & 1]
+
+    read = zero
+    for s in range(SLOTS):
+        read = jnp.where(sub == s, nt(c_out, scomb[s]), read)
+    columns = jnp.concatenate([grown, decay, jnp.zeros((96, 128), F32)], axis=0).T
+    for s in range(SLOTS):
+        old = scomb[s].astype(F32)
+        new = columns[:, 16 + s : 17 + s] * old + columns[:, s : s + 1] * b_in[s : s + 1].astype(F32)
+        stn[s] = new.astype(BF16)
+    own_states = pl.ds(0, SLOTS)
+    state_copy_out = pltpu.make_async_copy(stn.at[own_states], state_out.at[own_states], out_sem.at[2])
+    state_copy_out.start()
+    b_dot_c = jnp.sum(b_in.astype(F32) * c_out.astype(F32), axis=1, keepdims=True)
+    loads[5].wait()
+    loads[6].wait()
 
     wait_pieces(1)
 
@@ -419,14 +507,10 @@
         return carry
 
     lax.fori_loop(0, MOVES, paste_states, 0)
-    read = zero
-    for s in range(SLOTS):
-        read = jnp.where(sub == s, nt(c_out, scomb[places[s]]), read)
-    b_dot_c = jnp.sum(b_in.astype(F32) * c_out.astype(F32), axis=1, keepdims=True)
+    for k in range(MOVES):
+        read = jnp.where(sub == slots[k], nt(c_out, scomb[SLOTS + k]), read)
     readout = decay * read + grown * b_dot_c + head_lanes(dskip) * value_act
     gated = (readout * silu(gate_in)).astype(BF16)
-    loads[5].wait()
-    loads[6].wait()
     out_terms = nn(gated, wssm_v[...])
 
     away_a = recv_a.at[pl.ds(1, COLS - 1)]
@@ -439,7 +523,7 @@
     for d in range(COLS):
         part = recv_a[d]
         gathered = gathered + part * jnp.exp(part[:, HP : HP + 1] - top)
-    attended = (gathered / gathered[:, HP + 1 : HP + 2]).astype(BF16)
+    attended = jnp.where(real, gathered / gathered[:, HP + 1 : HP + 2], 0.0).astype(BF16)
     out_terms = out_terms + nn(attended[:, :HP], wattn_v[...])
     for c in range(COLS):
         send_o[c] = out_terms[:, 128 * c : 128 * (c + 1)].astype(BF16)
@@ -454,13 +538,16 @@
     lax.fori_loop(1, COLS, project, 0)
     recv_o[0] = send_o[col]
 
-    columns = jnp.concatenate([grown, decay, jnp.zeros((96, 128), F32)], axis=0).T
-    for s in range(SLOTS):
-        old = scomb[places[s]].astype(F32)
-        new = columns[:, 16 + s : 17 + s] * old + columns[:, s : s + 1] * b_in[s : s + 1].astype(F32)
-        stn[s] = new.astype(BF16)
-    state_copy_out = pltpu.make_async_copy(stn, state_out, out_sem.at[1])
-    state_copy_out.start()
+    lanes = lax.broadcasted_iota(I32, (128, 128), 1)
+    rows_b = lax.broadcasted_iota(I32, (16, 256), 0)
+    for k in range(MOVES):
+        up = jnp.sum(jnp.where(lanes == slots[k], columns, 0.0), axis=1, keepdims=True)
+        down_by = jnp.sum(jnp.where(lanes == slots[k] + 16, columns, 0.0), axis=1, keepdims=True)
+        b_row = jnp.sum(jnp.where(rows_b == slots[k], b_in.astype(F32), 0.0), axis=0, keepdims=True)
+        stn[SLOTS + k] = (down_by * scomb[SLOTS + k].astype(F32) + up * b_row).astype(BF16)
+    new_states = pl.ds(SLOTS, MOVES)
+    state_copy2 = pltpu.make_async_copy(stn.at[new_states], state_out.at[new_states], out_sem.at[3])
+    state_copy2.start()
 
     away_o = recv_o.at[pl.ds(1, COLS - 1)]
     pltpu.make_async_copy(away_o, away_o, ro_sem).wait()
@@ -477,21 +564,32 @@
     pltpu.make_async_copy(sent_r, sent_r, sr_sem).wait()
     sent_b = send_b.at[pl.ds(0, 3)]
     pltpu.make_async_copy(sent_b, sent_b, sb_sem).wait()
-    for sem, ref in ((ss_sem, recv_s), (sa_sem, send_a), (so_sem, send_o)):
+    for sem, ref in ((ss_sem, recv_s), (sa_sem, recv_a), (so_sem, send_o)):
         sent = ref.at[pl.ds(0, COLS - 1)]
         pltpu.make_async_copy(sent, sent, sem).wait()
-    kv_copy.wait()
-    state_copy_out.wait()
-
-
-def emit_kernel(*refs):
+    for copy in (kv_copy, kv_copy2, state_copy_out, state_copy2):
+        copy.wait()
+
+
+def emit_kernel(ms, pt, *refs):
     made, out, held, sem = refs[:5], refs[5:10], refs[10:15], refs[15]
+    row = lax.axis_index("rows")
+    ready = list(held)
+    ready[0] = held[0].at[pl.ds(0, 26)]
+    ready[1] = held[1].at[pl.ds(0, SLOTS)]
     reads = [pltpu.make_async_copy(made[i], held[i], sem.at[i]) for i in range(5)]
-    writes = [pltpu.make_async_copy(held[i], out[i], sem.at[5 + i]) for i in range(5)]
+    writes = [pltpu.make_async_copy(ready[i], out[i], sem.at[5 + i]) for i in range(5)]
     for read in reads:
         read.start()
     for i in (2, 3, 4, 0, 1):
         reads[i].wait()
+        for k in range(MOVES):
+            slot = ms[k, row]
+            if i == 0:
+                held[0][pt[0, slot]] = held[0][26 + 2 * k]
+                held[0][pt[1, slot]] = held[0][27 + 2 * k]
+            if i == 1:
+                held[1][slot] = held[1][SLOTS + k]
         writes[i].start()
     for write in writes:
         write.wait()
@@ -518,34 +616,37 @@
     tile = lambda *lead: pltpu.VMEM((*lead, 16, 128), BF16)
     made = pl.pallas_call(
         mixer_kernel,
-        out_shape=results,
+        out_shape=(
+            jax.ShapeDtypeStruct((34, PAGE, 512), BF16),
+            jax.ShapeDtypeStruct((SLOTS + MOVES, 128, NS), BF16),
+            *results[2:],
+        ),
         in_specs=[smem] * 7 + [vmem] * 9 + [anywhere] * 9,
         out_specs=(anywhere, anywhere, vmem, vmem, vmem),
         scratch_shapes=[
-            tile(ROWS, 5),
-            tile(ROWS, 5),
+            tile(ROWS, MOVES),
+            tile(ROWS, MOVES),
             tile(ROWS, MOVES),
             tile(ROWS, MOVES),
             pltpu.VMEM((34, PAGE, 512), BF16),
             pltpu.VMEM((SLOTS + MOVES, 128, NS), BF16),
-            pltpu.VMEM((26, PAGE, 512), BF16),
-            pltpu.VMEM((SLOTS, 128, NS), BF16),
-            tile(16),
-            pltpu.VMEM((16, 16, 128), F32),
+            pltpu.VMEM((34, PAGE, 512), BF16),
+            pltpu.VMEM((SLOTS + MOVES, 128, NS), BF16),
+            pltpu.VMEM((16, 8, 128), F32),
+            pltpu.VMEM((8, 16, 128), F32),
+            pltpu.VMEM((4, 32, 128), F32),
+            pltpu.VMEM((ROWS, 8, 128), F32),
             pltpu.VMEM((8, 128), I32),
             pltpu.SMEM((8, 128), I32),
-            tile(8, 12),
-            tile(8, 12),
-            tile(4, 3),
-            tile(4, 3),
+            tile(8, 13),
+            tile(8, 13),
+            tile(4, 5),
+            tile(4, 5),
             tile(),
             tile(COLS),
             pltpu.VMEM((16, 8, 256), F32),
             pltpu.VMEM((16, 1, 512), F32),
-            pltpu.VMEM((8, 16, 128), F32),
-            pltpu.VMEM((8, 16, 128), F32),
-            pltpu.VMEM((8, 16, 128), F32),
-            pltpu.VMEM((COLS, 16, 128), F32),
+            pltpu.VMEM((8, 2, 16, 128), F32),
             pltpu.VMEM((COLS, 16, 128), F32),
             tile(COLS),
             tile(COLS),
@@ -559,7 +660,7 @@
         + [dma] * 3
         + [dma((2,))]
         + [dma] * 10
-        + [dma((9,)), dma, dma((2,))],
+        + [dma((9,)), dma, dma((4,))],
         compiler_params=pltpu.CompilerParams(
             collective_id=0, has_side_effects=True, vmem_limit_bytes=60 * 1024 * 1024
         ),
@@ -574,11 +675,11 @@
     kv_next, state_next, mixed, cx, cbc = pl.pallas_call(
         emit_kernel,
         out_shape=results,
-        in_specs=[anywhere] * 5,
+        in_specs=[smem] * 2 + [anywhere] * 5,
         out_specs=(anywhere,) * 5,
-        scratch_shapes=[pltpu.VMEM(r.shape, r.dtype) for r in results] + [dma((10,))],
+        scratch_shapes=[pltpu.VMEM(m.shape, m.dtype) for m in made] + [dma((10,))],
         name="emit",
-    )(*made)
+    )(ms, pt, *made)
     return (
         mixed,
         state_next.reshape(SLOTS, 2, HP, NS),

time: 68.4 us -> 63.7 us (0.931); the launches traced: 68.1 us -> 62.6 us
  Pallas kernels: 67.5 us -> 62 us
    pallas_call x2, Pallas kernels: 67.5 us -> 62 us  [the longest x1 58.5 us: local(): pl.pallas_call(mixer_kernel, out_shape=(jax.ShapeDtypeStruct((34, PAGE, 5...]
where the time goes in v3:
time: 63.7 us; the launch traced here: 62.6 us
  Pallas kernels  62 us (97%)
  between operations  0.65 us (1%)
    pallas_call x1, Pallas kernels, local(): pl.pallas_call(mixer_kernel, out_shape=(jax.ShapeDtypeStruct((34, PAGE, 5...  58.5 us
    pallas_call x1, Pallas kernels, local(): pl.pallas_call(emit_kernel, out_shape=results, in_specs=[smem] * 2 + [any...  3.52 us

profile of v3, /device:TPU:6, one launch (start us, length us, event | category | flops | bytes accessed | tf_op | source)
XLA Modules:
  0.0 62.6 jit_solution(5822894168111879438)
XLA Ops:
  0.6 58.5 %mixer.1 = (bf16[34,32,512]{2,1,0:T(8,128)(2,1)}, bf16[17,128,256]{2,1,0:T(8,128)(2,1)}, bf16[13,128]{1,0:T(8,128)(2,1)}, bf16[3,13,128]{2,1,0:T(8,128)(2,1)}, bf16[3,13,512]{2,1,0:T(8,128)(2,1)}) custom-call(s32[4,32]{1,0:T(4,128)} %bitcast.23, s32[4,32]{1,0:T(4,128)} %bitcast.27, s32[416]{0:T(512)} %lengths.1, s32[2,13]{1,0:T(2,128)} %bitcast.29, f32[2]{0:T(128)} %dtb.1, ...), custom_call_target="tpu_custom_call" | custom-call | tf_op jit(solution)/shard_map/mixer/pallas_call | solution.py:617
  59.1 3.5 %emit.1 = (bf16[26,32,512]{2,1,0:T(8,128)(2,1)}, bf16[13,128,256]{2,1,0:T(8,128)(2,1)}, bf16[13,128]{1,0:T(8,128)(2,1)}, bf16[3,13,128]{2,1,0:T(8,128)(2,1)}, bf16[3,13,512]{2,1,0:T(8,128)(2,1)}) custom-call(s32[4,32]{1,0:T(4,128)} %bitcast.25, s32[2,13]{1,0:T(2,128)} %bitcast.30, bf16[34,32,512]{2,1,0:T(8,128)(2,1)} %get-tuple-element.15.refs_0_, ...), custom_call_target="tpu_custom_call" | custom-call | tf_op jit(solution)/shard_map/emit/pallas_call | solution.py:675

commit v4 on v3

--- a/solution.py
+++ b/solution.py
@@ -96,9 +96,12 @@
 
     pl.semaphore_wait(barrier, ROWS + COLS - 2)
 
+    def far_first(j, half):
+        return half + jnp.where((j & 1) == 1, (j + 1) >> 1, -(j >> 1))
+
     def hop1(kind):
         def send(d, carry):
-            to = 2 * ((chip + d) & 15) + kind
+            to = 2 * ((chip + far_first(d, 8)) & 15) + kind
 
             @pl.when(to != row)
             def _():
@@ -122,10 +125,6 @@
 
     loads[4].wait()
     lax.fori_loop(0, MOVES, cut_states, 0)
-
-    @pl.when(core == 1)
-    def _():
-        hop1(1)
 
     lane = lax.broadcasted_iota(I32, (128, 128), 1)
     sub = lax.broadcasted_iota(I32, (128, 128), 0)
@@ -218,6 +217,10 @@
 
     lax.fori_loop(1, 8, reduce_in, 0)
 
+    @pl.when(core == 1)
+    def _():
+        hop1(1)
+
     recv_r[0] = send_r[member]
 
     load_table.wait()
@@ -255,8 +258,10 @@
             send2[t, k] = recv1[(code >> 3) & (ROWS - 1), code & 3]
         return carry
 
-    def hop2(d, carry):
+    def hop2(j, carry):
+        d = far_first(j, 16)
         to = (row + d) & (ROWS - 1)
+        pick(to, carry)
         pltpu.make_async_remote_copy(
             send2.at[to], recv2.at[d], s2_sem, r2_sem.at[core], device_id=(to, col), device_id_type=MESH
         ).start()
@@ -267,8 +272,8 @@
         def _():
             recv1[0] = send1[row]
             pltpu.make_async_copy(away1, away1, r1_sem).wait()
-            lax.fori_loop(0, ROWS, pick, 0)
-            lax.fori_loop(1, ROWS, hop2, 0)
+            lax.fori_loop(0, ROWS - 1, hop2, 0)
+            pick(row, 0)
             recv2[0] = send2[row]
 
     second_hop(0)
@@ -319,14 +324,15 @@
             bc_rows = jnp.where((sub == SLOTS + k) & (quarter == m), moved, bc_rows)
     send_s[...] = jnp.where(real, sum_s / root, bc_rows).astype(BF16)
 
-    def share(d, carry):
+    def share(j, carry):
+        d = far_first(j, 8)
         to = (col + d) & (COLS - 1)
         pltpu.make_async_remote_copy(
             send_s, recv_s.at[d], ss_sem, rs_sem, device_id=(row, to), device_id_type=MESH
         ).start()
         return carry
 
-    lax.fori_loop(1, COLS, share, 0)
+    lax.fori_loop(0, COLS - 1, share, 0)
     recv_s[0] = send_s[...]
 
     second_hop(1)
@@ -473,14 +479,15 @@
                 tile = jnp.where(sub == slots[k], jnp.broadcast_to(found[k][half][h : h + 1], (16, 128)), tile)
             send_a[h, half] = tile
 
-    def attend(d, carry):
+    def attend(j, carry):
+        d = far_first(j, 8)
         to = (col + d) & (COLS - 1)
         pltpu.make_async_remote_copy(
             send_a.at[to >> 1, to & 1], recv_a.at[d], sa_sem, ra_sem, device_id=(row, to), device_id_type=MESH
         ).start()
         return carry
 
-    lax.fori_loop(1, COLS, attend, 0)
+    lax.fori_loop(0, COLS - 1, attend, 0)
     recv_a[0] = send_a[col >> 1, col & 1]
 
     read = zero
@@ -528,14 +535,15 @@
     for c in range(COLS):
         send_o[c] = out_terms[:, 128 * c : 128 * (c + 1)].astype(BF16)
 
-    def project(d, carry):
+    def project(j, carry):
+        d = far_first(j, 8)
         to = (col + d) & (COLS - 1)
         pltpu.make_async_remote_copy(
             send_o.at[to], recv_o.at[d], so_sem, ro_sem, device_id=(row, to), device_id_type=MESH
         ).start()
         return carry
 
-    lax.fori_loop(1, COLS, project, 0)
+    lax.fori_loop(0, COLS - 1, project, 0)
     recv_o[0] = send_o[col]
 
     lanes = lax.broadcasted_iota(I32, (128, 128), 1)

time: 63.7 us -> 63.4 us (level)
  the two profiles are of different devices: /device:TPU:6 before, /device:TPU:1 now
where the time goes in v4:
time: 63.4 us; the launch traced here: 63.2 us
  Pallas kernels  62.5 us (99%)
  between operations  0.65 us (1%)
    pallas_call x1, Pallas kernels, local(): pl.pallas_call(mixer_kernel, out_shape=(jax.ShapeDtypeStruct((34, PAGE, 5...  59 us
    pallas_call x1, Pallas kernels, local(): pl.pallas_call(emit_kernel, out_shape=results, in_specs=[smem] * 2 + [any...  3.52 us

profile of v4, /device:TPU:1, one launch (start us, length us, event | category | flops | bytes accessed | tf_op | source)
XLA Modules:
  0.0 63.2 jit_solution(6223971683793344658)
XLA Ops:
  0.6 59.0 %mixer.1 = (bf16[34,32,512]{2,1,0:T(8,128)(2,1)}, bf16[17,128,256]{2,1,0:T(8,128)(2,1)}, bf16[13,128]{1,0:T(8,128)(2,1)}, bf16[3,13,128]{2,1,0:T(8,128)(2,1)}, bf16[3,13,512]{2,1,0:T(8,128)(2,1)}) custom-call(s32[4,32]{1,0:T(4,128)} %bitcast.23, s32[4,32]{1,0:T(4,128)} %bitcast.27, s32[416]{0:T(512)} %lengths.1, s32[2,13]{1,0:T(2,128)} %bitcast.29, f32[2]{0:T(128)} %dtb.1, ...), custom_call_target="tpu_custom_call" | custom-call | tf_op jit(solution)/shard_map/mixer/pallas_call | solution.py:625
  59.7 3.5 %emit.1 = (bf16[26,32,512]{2,1,0:T(8,128)(2,1)}, bf16[13,128,256]{2,1,0:T(8,128)(2,1)}, bf16[13,128]{1,0:T(8,128)(2,1)}, bf16[3,13,128]{2,1,0:T(8,128)(2,1)}, bf16[3,13,512]{2,1,0:T(8,128)(2,1)}) custom-call(s32[4,32]{1,0:T(4,128)} %bitcast.25, s32[2,13]{1,0:T(2,128)} %bitcast.30, bf16[34,32,512]{2,1,0:T(8,128)(2,1)} %get-tuple-element.15.refs_0_, ...), custom_call_target="tpu_custom_call" | custom-call | tf_op jit(solution)/shard_map/emit/pallas_call | solution.py:683

commit v5 on v4

--- a/solution.py
+++ b/solution.py
@@ -41,7 +41,7 @@
     kv_out, state_out, mixed_out, cx_out, cbc_out,
     send1, recv1, send2, recv2, pcomb, scomb, kvn, stn, leave, going, passing, came, table_v, table,
     send_r, recv_r, send_b, recv_b, send_s, recv_s, qbuf, fresh,
-    send_a, recv_a, send_o, recv_o, tokens_v, wz_v, wx_v, shared_v, wssm_v, wattn_v,
+    send_a, leave_a, recv_a, send_o, recv_o, tokens_v, wz_v, wx_v, shared_v, wssm_v, wattn_v,
     s1_sem, r1_sem, s2_sem, r2_sem, sr_sem, rr_sem, sb_sem, rb_sem, ss_sem, rs_sem,
     sa_sem, ra_sem, so_sem, ro_sem, in_sem, table_sem, out_sem,
 ):
@@ -448,7 +448,11 @@
         weights = jnp.where(live, jnp.exp(scores - peak), 0.0)
         summed = nn(weights.astype(BF16), both[:, 256:])
         summed = jnp.where(head < 4, summed[:, :128], summed[:, 128:])
-        stats = jnp.where(lane8 == HP, peak, jnp.sum(weights, axis=1, keepdims=True))
+        rounded = peak.astype(BF16).astype(F32)
+        rest = (peak - rounded).astype(BF16).astype(F32)
+        stats = jnp.where(lane8 == HP, rounded, jnp.sum(weights, axis=1, keepdims=True))
+        stats = jnp.where(lane8 == HP + 1, rest, stats)
+        stats = jnp.where(lane8 == HP + 2, peak - rounded - rest, stats)
         return jnp.where(lane8 < HP, summed, stats), jnp.where(lane8 < HP, pltpu.roll(summed, HP, 1), stats)
 
     for s in range(SLOTS):
@@ -477,18 +481,18 @@
             tile = send_a[h, half]
             for k in range(MOVES):
                 tile = jnp.where(sub == slots[k], jnp.broadcast_to(found[k][half][h : h + 1], (16, 128)), tile)
-            send_a[h, half] = tile
+            leave_a[h, half] = tile.astype(BF16)
 
     def attend(j, carry):
         d = far_first(j, 8)
         to = (col + d) & (COLS - 1)
         pltpu.make_async_remote_copy(
-            send_a.at[to >> 1, to & 1], recv_a.at[d], sa_sem, ra_sem, device_id=(row, to), device_id_type=MESH
+            leave_a.at[to >> 1, to & 1], recv_a.at[d], sa_sem, ra_sem, device_id=(row, to), device_id_type=MESH
         ).start()
         return carry
 
     lax.fori_loop(0, COLS - 1, attend, 0)
-    recv_a[0] = send_a[col >> 1, col & 1]
+    recv_a[0] = leave_a[col >> 1, col & 1]
 
     read = zero
     for s in range(SLOTS):
@@ -522,15 +526,15 @@
 
     away_a = recv_a.at[pl.ds(1, COLS - 1)]
     pltpu.make_async_copy(away_a, away_a, ra_sem).wait()
-    top = recv_a[0]
-    for d in range(1, COLS):
-        top = jnp.maximum(top, recv_a[d])
-    top = top[:, HP : HP + 1]
+    parts = [recv_a[d].astype(F32) for d in range(COLS)]
+    peaks = [part[:, HP : HP + 1] + part[:, HP + 1 : HP + 2] + part[:, HP + 2 : HP + 3] for part in parts]
+    top = peaks[0]
+    for peak in peaks[1:]:
+        top = jnp.maximum(top, peak)
     gathered = zero
-    for d in range(COLS):
-        part = recv_a[d]
-        gathered = gathered + part * jnp.exp(part[:, HP : HP + 1] - top)
-    attended = jnp.where(real, gathered / gathered[:, HP + 1 : HP + 2], 0.0).astype(BF16)
+    for part, peak in zip(parts, peaks):
+        gathered = gathered + part * jnp.exp(peak - top)
+    attended = jnp.where(real, gathered / gathered[:, HP + 3 : HP + 4], 0.0).astype(BF16)
     out_terms = out_terms + nn(attended[:, :HP], wattn_v[...])
     for c in range(COLS):
         send_o[c] = out_terms[:, 128 * c : 128 * (c + 1)].astype(BF16)
@@ -655,7 +659,8 @@
             pltpu.VMEM((16, 8, 256), F32),
             pltpu.VMEM((16, 1, 512), F32),
             pltpu.VMEM((8, 2, 16, 128), F32),
-            pltpu.VMEM((COLS, 16, 128), F32),
+            tile(8, 2),
+            tile(COLS),
             tile(COLS),
             tile(COLS),
             pltpu.VMEM((64, 416), BF16),

time: 63.4 us -> 63.3 us (level)
  no operation moved by 1% of the time
where the time goes in v5:
time: 63.3 us; the launch traced here: 63.1 us
  Pallas kernels  62.4 us (99%)
  between operations  0.65 us (1%)
    pallas_call x1, Pallas kernels, local(): pl.pallas_call(mixer_kernel, out_shape=(jax.ShapeDtypeStruct((34, PAGE, 5...  58.9 us
    pallas_call x1, Pallas kernels, local(): pl.pallas_call(emit_kernel, out_shape=results, in_specs=[smem] * 2 + [any...  3.52 us

profile of v5, /device:TPU:1, one launch (start us, length us, event | category | flops | bytes accessed | tf_op | source)
XLA Modules:
  0.0 63.1 jit_solution(3578681151605545396)
XLA Ops:
  0.6 58.9 %mixer.1 = (bf16[34,32,512]{2,1,0:T(8,128)(2,1)}, bf16[17,128,256]{2,1,0:T(8,128)(2,1)}, bf16[13,128]{1,0:T(8,128)(2,1)}, bf16[3,13,128]{2,1,0:T(8,128)(2,1)}, bf16[3,13,512]{2,1,0:T(8,128)(2,1)}) custom-call(s32[4,32]{1,0:T(4,128)} %bitcast.23, s32[4,32]{1,0:T(4,128)} %bitcast.27, s32[416]{0:T(512)} %lengths.1, s32[2,13]{1,0:T(2,128)} %bitcast.29, f32[2]{0:T(128)} %dtb.1, ...), custom_call_target="tpu_custom_call" | custom-call | tf_op jit(solution)/shard_map/mixer/pallas_call | solution.py:629
  59.6 3.5 %emit.1 = (bf16[26,32,512]{2,1,0:T(8,128)(2,1)}, bf16[13,128,256]{2,1,0:T(8,128)(2,1)}, bf16[13,128]{1,0:T(8,128)(2,1)}, bf16[3,13,128]{2,1,0:T(8,128)(2,1)}, bf16[3,13,512]{2,1,0:T(8,128)(2,1)}) custom-call(s32[4,32]{1,0:T(4,128)} %bitcast.25, s32[2,13]{1,0:T(2,128)} %bitcast.30, bf16[34,32,512]{2,1,0:T(8,128)(2,1)} %get-tuple-element.15.refs_0_, ...), custom_call_target="tpu_custom_call" | custom-call | tf_op jit(solution)/shard_map/emit/pallas_call | solution.py:688
